TPU v7x, 32 devices: a whole 2x2x4 slice. The times are simulated.
32 devices in a mesh: dp: 8 (over z, x), tensor: 4 (over y, core).
Axes of the slice: x: 2, y: 2, z: 4, core: 2. Of those that a mesh axis runs over, the one named last changes fastest.
Arguments:
- tokens: bfloat16 [8192, 1024], P(('dp', 'tensor')), may hold values from -24 to 24
- cotangent: bfloat16 [8192, 1024], P(('dp', 'tensor')), may hold values from -6 to 6
- bucket_start: int32 [32], replicated, may hold values from 0 to 30, as said below
- w_qkv: bfloat16 [1024, 3072], P(('dp', 'tensor')), may hold values from -0.1875 to 0.1875
- w_out: bfloat16 [1024, 1024], P(('dp', 'tensor')), may hold values from -0.1875 to 0.1875
- s_qk: bfloat16 [1024], P(('dp', 'tensor')), may hold values from 0.796875 to 1.59375
- alpha_a: bfloat16 [1024], P(('dp', 'tensor')), may hold values from 0.14941406 to 0.59765625
- alpha_m: bfloat16 [1024], P(('dp', 'tensor')), may hold values from 0.14941406 to 0.59765625
- w_up: bfloat16 [1024, 4096], P('dp', 'tensor'), may hold values from -0.1875 to 0.1875
- w_gate: bfloat16 [1024, 4096], P('dp', 'tensor'), may hold values from -0.1875 to 0.1875
- w_down: bfloat16 [1024, 4096], P('dp', 'tensor'), may hold values from -0.09375 to 0.09375
- s_u: bfloat16 [4096], P('tensor'), may hold values from 0.5 to 2
- s_v: bfloat16 [4096], P('tensor'), may hold values from 0.5 to 2
Outputs:
- layer_out: bfloat16 [8192, 1024], P(('dp', 'tensor'))
- grad_tokens: bfloat16 [8192, 1024], P(('dp', 'tensor'))
- grad_w_qkv: float32 [1024, 3072], P(('dp', 'tensor'))
- grad_w_out: float32 [1024, 1024], P(('dp', 'tensor'))
- grad_s_qk: float32 [1024], P(('dp', 'tensor'))
- grad_alpha_a: float32 [1024], P(('dp', 'tensor'))
- grad_alpha_m: float32 [1024], P(('dp', 'tensor'))
- grad_w_up: float32 [1024, 4096], P('dp', 'tensor')
- grad_w_gate: float32 [1024, 4096], P('dp', 'tensor')
- grad_w_down: float32 [1024, 4096], P('dp', 'tensor')
- grad_s_u: float32 [4096], P('tensor')
- grad_s_v: float32 [4096], P('tensor')
- stream_rms: float32 [3], replicated
Inputs may be any that keep to these rules, and one draw needn't show every extreme that they name: Buckets are the aligned runs of 256 token rows, and groups the aligned runs of 4 buckets. A sequence is either all 4 buckets of a group or two buckets 2i and 2i + 1 of one group; bucket_start names the first bucket of the sequence. Half of the 8 groups, rounded up, are each one sequence; the last group is always made of two-bucket sequences, and which of the others are whole changes with the seed.
All inputs are finite; a program needn't handle non-finite values.
Results may differ from a plain program's by a relative error of at most 0.018.
Values may be sent and summed in bfloat16 or wider, within the bound.
A program may use at most 192 MiB of HBM per device.

v0:
```python
import math

import jax
import jax.numpy as jnp
from jax import lax
from jax.sharding import PartitionSpec as P

HEAD_DIM = 64


EPSILON = 1e-06
MASKED_SCORE = -1e30


def rms_rows(value):
    return value * lax.rsqrt(jnp.mean(value * value, axis=-1, keepdims=True) + EPSILON)


def rms_back(upstream, normed, source):
    factor = lax.rsqrt(jnp.mean(source * source, axis=-1, keepdims=True) + EPSILON)
    return factor * (upstream - normed * jnp.mean(upstream * normed, axis=-1, keepdims=True))


def unit_heads(value):
    shaped = value.reshape(value.shape[0], -1, HEAD_DIM)
    factor = lax.rsqrt(jnp.sum(shaped * shaped, axis=-1, keepdims=True) + EPSILON)
    return ((shaped * factor).reshape(value.shape), factor)


def unit_back(upstream, normed, factor):
    upper_grad = upstream.reshape(normed.shape[0], -1, HEAD_DIM)
    normed_heads = normed.reshape(normed.shape[0], -1, HEAD_DIM)
    result = factor * (
        upper_grad - normed_heads * jnp.sum(upper_grad * normed_heads, axis=-1, keepdims=True)
    )
    return result.reshape(upstream.shape)


def block_span(total_rows, row_count):
    units = total_rows // row_count
    block_units = max(1, min(units, 512 // row_count))
    while units % block_units:
        block_units -= 1
    return row_count * block_units


def local(
    tokens,
    cotangent,
    bucket_start,
    w_qkv,
    w_out,
    s_qk,
    alpha_a,
    alpha_m,
    w_up,
    w_gate,
    w_down,
    s_u,
    s_v,
):
    row_count, model_width = tokens.shape
    head_count = model_width // HEAD_DIM
    score_scale = math.sqrt(HEAD_DIM)
    spread = lax.axis_size("tensor")
    group_rows = spread * row_count
    tensor_slot = lax.axis_index("tensor")
    qkv_full, out_full, gain_qk, mix_attn, mix_mlp = (
        lax.all_gather(w_qkv, ("dp", "tensor"), axis=0, tiled=True),
        lax.all_gather(w_out, ("dp", "tensor"), axis=0, tiled=True),
        lax.all_gather(s_qk, ("dp", "tensor"), axis=0, tiled=True),
        lax.all_gather(alpha_a, ("dp", "tensor"), axis=0, tiled=True),
        lax.all_gather(alpha_m, ("dp", "tensor"), axis=0, tiled=True),
    )
    up_full, gate_full, down_full = (
        lax.all_gather(w_up, "dp", axis=0, tiled=True),
        lax.all_gather(w_gate, "dp", axis=0, tiled=True),
        lax.all_gather(w_down, "dp", axis=0, tiled=True),
    )
    gain_qk = gain_qk.astype(jnp.float32)
    mix_attn = mix_attn.astype(jnp.float32)
    mix_mlp = mix_mlp.astype(jnp.float32)
    scale_up = s_u.astype(jnp.float32)
    scale_gate = s_v.astype(jnp.float32)
    starts = lax.dynamic_slice_in_dim(bucket_start, lax.axis_index("dp") * spread, spread)
    key_seq = jnp.repeat(starts, row_count)
    own_seq = starts[tensor_slot]
    query_pos = tensor_slot * row_count + jnp.arange(row_count, dtype=jnp.int32)

    def allowed(key_start, key_count):
        key_pos = key_start + jnp.arange(key_count, dtype=jnp.int32)
        seq_part = lax.dynamic_slice_in_dim(key_seq, key_start, key_count)
        return (key_pos[None, :] <= query_pos[:, None]) & (seq_part[None, :] == own_seq)

    inputs = tokens.astype(jnp.float32)
    qkv = jnp.dot(tokens, qkv_full, preferred_element_type=jnp.float32)
    q_unit, q_factor = unit_heads(qkv[:, :model_width])
    k_unit, k_factor = unit_heads(qkv[:, model_width : 2 * model_width])
    query_low = (q_unit * gain_qk).astype(jnp.bfloat16)
    keys_low = (k_unit * gain_qk).astype(jnp.bfloat16)
    values_low = qkv[:, 2 * model_width :].astype(jnp.bfloat16)
    query_heads = query_low.reshape(row_count, head_count, HEAD_DIM)
    key_all, value_all = (
        lax.all_gather(keys_low, "tensor", axis=0, tiled=True),
        lax.all_gather(values_low, "tensor", axis=0, tiled=True),
    )
    key_block = block_span(group_rows, row_count)
    blocks = group_rows // key_block

    def block_scores(key_source, key_start, key_count):
        key_part = lax.dynamic_slice_in_dim(key_source, key_start, key_count).reshape(
            key_count, head_count, HEAD_DIM
        )
        return (
            jnp.einsum("qhd,khd->hqk", query_heads, key_part, preferred_element_type=jnp.float32)
            * score_scale
        )

    def stat_step(state_pair, block_index):
        row_top, row_total = state_pair
        key_start = block_index * key_block
        allowed_keys = allowed(key_start, key_block)[None]
        masked = jnp.where(allowed_keys, block_scores(key_all, key_start, key_block), MASKED_SCORE)
        new_top = jnp.maximum(row_top, jnp.max(masked, axis=-1))
        fresh = jnp.where(allowed_keys, jnp.exp(masked - new_top[..., None]), 0.0)
        row_total = row_total * jnp.exp(row_top - new_top) + jnp.sum(fresh, axis=-1)
        return ((new_top, row_total), None)

    start_state = (
        jnp.full((head_count, row_count), MASKED_SCORE, jnp.float32),
        jnp.zeros((head_count, row_count), jnp.float32),
    )
    (row_top, row_total), _ = lax.scan(stat_step, start_state, jnp.arange(blocks))
    log_total = row_top + jnp.log(row_total)

    def probs_for(key_source, key_start, key_count):
        scores = block_scores(key_source, key_start, key_count)
        allowed_keys = allowed(key_start, key_count)[None]
        return jnp.where(allowed_keys, jnp.exp(scores - log_total[..., None]), 0.0)

    def value_part(value_source, key_start, key_count):
        return lax.dynamic_slice_in_dim(value_source, key_start, key_count).reshape(
            key_count, head_count, HEAD_DIM
        )

    def out_step(carry_sum, block_index):
        key_start = block_index * key_block
        attn_probs = probs_for(key_all, key_start, key_block).astype(jnp.bfloat16)
        term = jnp.einsum(
            "hqk,khd->qhd",
            attn_probs,
            value_part(value_all, key_start, key_block),
            preferred_element_type=jnp.float32,
        )
        return (carry_sum + term, None)

    attended, _ = lax.scan(
        out_step, jnp.zeros((row_count, head_count, HEAD_DIM), jnp.float32), jnp.arange(blocks)
    )
    attended_low = attended.reshape(row_count, model_width).astype(jnp.bfloat16)
    branch_a = jnp.dot(attended_low, out_full, preferred_element_type=jnp.float32)
    h_attn = rms_rows(branch_a)
    resid_one = inputs + mix_attn * (h_attn - inputs)
    hidden_one = rms_rows(resid_one)
    hidden_low = hidden_one.astype(jnp.bfloat16)
    rows_all = lax.all_gather(hidden_low, "tensor", axis=0, tiled=True)
    up_raw = jnp.dot(rows_all, up_full, preferred_element_type=jnp.float32)
    gate_raw = jnp.dot(rows_all, gate_full, preferred_element_type=jnp.float32)
    up_scaled = up_raw * scale_up
    gate_scaled = gate_raw * scale_gate
    gate_sigmoid = jax.nn.sigmoid(gate_scaled)
    silu_gate = gate_scaled * gate_sigmoid
    inner_low = (up_scaled * silu_gate).astype(jnp.bfloat16)
    branch_m = lax.psum_scatter(
        jnp.einsum("tf,df->td", inner_low, down_full, preferred_element_type=jnp.float32).astype(
            jnp.bfloat16
        ),
        "tensor",
        scatter_dimension=0,
        tiled=True,
    ).astype(jnp.float32)
    h_mlp = rms_rows(branch_m)
    resid_two = hidden_one + mix_mlp * (h_mlp - hidden_one)
    result = rms_rows(resid_two)
    partial_stats = jnp.stack(
        [jnp.sum(branch_a * branch_a), jnp.sum(branch_m * branch_m), jnp.sum(resid_two * resid_two)]
    )
    upstream = cotangent.astype(jnp.float32)
    d_resid_two = rms_back(upstream, result, resid_two)
    grad_mix_mlp = jnp.sum(d_resid_two * (h_mlp - hidden_one), axis=0)
    d_branch_m = rms_back(mix_mlp * d_resid_two, h_mlp, branch_m).astype(jnp.bfloat16)
    grads_all = lax.all_gather(d_branch_m, "tensor", axis=0, tiled=True)
    d_inner = jnp.dot(grads_all, down_full, preferred_element_type=jnp.float32)
    grad_up_scaled = d_inner * silu_gate
    grad_gate_scaled = (
        d_inner * up_scaled * gate_sigmoid * (1.0 + gate_scaled * (1.0 - gate_sigmoid))
    )
    grad_scale_up = jnp.sum(grad_up_scaled * up_raw, axis=0)
    grad_scale_gate = jnp.sum(grad_gate_scaled * gate_raw, axis=0)
    up_grad_low = (grad_up_scaled * scale_up).astype(jnp.bfloat16)
    gate_grad_low = (grad_gate_scaled * scale_gate).astype(jnp.bfloat16)
    grad_down = jnp.einsum("td,tf->df", grads_all, inner_low, preferred_element_type=jnp.float32)
    grad_up = jnp.einsum("td,tf->df", rows_all, up_grad_low, preferred_element_type=jnp.float32)
    grad_gate = jnp.einsum("td,tf->df", rows_all, gate_grad_low, preferred_element_type=jnp.float32)
    first = jnp.einsum("tf,df->td", up_grad_low, up_full, preferred_element_type=jnp.float32)
    d_hidden_one = (1.0 - mix_mlp) * d_resid_two + lax.psum_scatter(
        (
            first
            + jnp.einsum("tf,df->td", gate_grad_low, gate_full, preferred_element_type=jnp.float32)
        ).astype(jnp.bfloat16),
        "tensor",
        scatter_dimension=0,
        tiled=True,
    ).astype(jnp.float32)
    d_resid_one = rms_back(d_hidden_one, hidden_one, resid_one)
    grad_mix_attn = jnp.sum(d_resid_one * (h_attn - inputs), axis=0)
    d_branch_a = rms_back(mix_attn * d_resid_one, h_attn, branch_a).astype(jnp.bfloat16)
    grad_out = jnp.einsum("tc,td->cd", attended_low, d_branch_a, preferred_element_type=jnp.float32)
    d_attended = jnp.einsum(
        "td,cd->tc", d_branch_a, out_full, preferred_element_type=jnp.float32
    ).astype(jnp.bfloat16)
    d_heads = d_attended.reshape(row_count, head_count, HEAD_DIM)
    row_delta = jnp.sum(d_heads.astype(jnp.float32) * attended, axis=-1).T
    key_back, value_back = (
        lax.all_gather(keys_low, "tensor", axis=0, tiled=True),
        lax.all_gather(values_low, "tensor", axis=0, tiled=True),
    )

    def score_grads(key_start, key_count):
        attn_probs = probs_for(key_back, key_start, key_count)
        d_probs = jnp.einsum(
            "qhd,khd->hqk",
            d_heads,
            value_part(value_back, key_start, key_count),
            preferred_element_type=jnp.float32,
        )
        d_scores = (attn_probs * (d_probs - row_delta[..., None])).astype(jnp.bfloat16)
        return (attn_probs, d_scores)

    def query_step(carry_sum, block_index):
        key_start = block_index * key_block
        attn_probs, d_scores = score_grads(key_start, key_block)
        key_part = lax.dynamic_slice_in_dim(key_back, key_start, key_block).reshape(
            key_block, head_count, HEAD_DIM
        )
        return (
            carry_sum
            + jnp.einsum("hqk,khd->qhd", d_scores, key_part, preferred_element_type=jnp.float32),
            None,
        )

    d_query, _ = lax.scan(
        query_step, jnp.zeros((row_count, head_count, HEAD_DIM), jnp.float32), jnp.arange(blocks)
    )
    d_query = d_query.reshape(row_count, model_width) * score_scale
    part_rows = lax.axis_size("tensor") * row_count
    sub_block = block_span(part_rows, row_count)

    def one_block(block_index):
        begin = block_index * sub_block
        attn_probs, d_scores = score_grads(begin, sub_block)
        d_keys = (
            jnp.einsum("hqk,qhd->khd", d_scores, query_heads, preferred_element_type=jnp.float32)
            * score_scale
        )
        d_values = jnp.einsum(
            "hqk,qhd->khd",
            attn_probs.astype(jnp.bfloat16),
            d_heads,
            preferred_element_type=jnp.float32,
        )
        return jnp.concatenate(
            [d_keys.reshape(sub_block, model_width), d_values.reshape(sub_block, model_width)],
            axis=1,
        )

    block_terms = lax.map(one_block, jnp.arange(part_rows // sub_block))
    key_grads = lax.psum_scatter(
        block_terms.reshape(part_rows, 2 * model_width).astype(jnp.bfloat16),
        "tensor",
        scatter_dimension=0,
        tiled=True,
    ).astype(jnp.float32)
    d_keys_own = key_grads[:, :model_width]
    d_values_own = key_grads[:, model_width:]
    grad_gain = jnp.sum(d_query * q_unit + d_keys_own * k_unit, axis=0)
    d_qkv = jnp.concatenate(
        [
            unit_back(d_query * gain_qk, q_unit, q_factor),
            unit_back(d_keys_own * gain_qk, k_unit, k_factor),
            d_values_own,
        ],
        axis=1,
    ).astype(jnp.bfloat16)
    grad_qkv = jnp.einsum("tc,tf->cf", tokens, d_qkv, preferred_element_type=jnp.float32)
    d_tokens = (1.0 - mix_attn) * d_resid_one + jnp.einsum(
        "tf,cf->tc", d_qkv, qkv_full, preferred_element_type=jnp.float32
    )
    sum_qkv, sum_out, sum_gain, sum_mix_attn, sum_mix_mlp = (
        lax.psum_scatter(grad_qkv, ("dp", "tensor"), scatter_dimension=0, tiled=True),
        lax.psum_scatter(grad_out, ("dp", "tensor"), scatter_dimension=0, tiled=True),
        lax.psum_scatter(grad_gain, ("dp", "tensor"), scatter_dimension=0, tiled=True),
        lax.psum_scatter(grad_mix_attn, ("dp", "tensor"), scatter_dimension=0, tiled=True),
        lax.psum_scatter(grad_mix_mlp, ("dp", "tensor"), scatter_dimension=0, tiled=True),
    )
    sum_up, sum_gate, sum_down = (
        lax.psum_scatter(
            grad_up.astype(jnp.bfloat16), "dp", scatter_dimension=0, tiled=True
        ).astype(jnp.float32),
        lax.psum_scatter(
            grad_gate.astype(jnp.bfloat16), "dp", scatter_dimension=0, tiled=True
        ).astype(jnp.float32),
        lax.psum_scatter(
            grad_down.astype(jnp.bfloat16), "dp", scatter_dimension=0, tiled=True
        ).astype(jnp.float32),
    )
    sum_scale_up, sum_scale_gate = lax.psum((grad_scale_up, grad_scale_gate), "dp")
    stat_sums = lax.psum(partial_stats, ("dp", "tensor"))
    entry_count = row_count * model_width * lax.axis_size("dp") * spread
    stream_rms = jnp.sqrt(stat_sums / entry_count)
    return (
        result.astype(jnp.bfloat16),
        d_tokens.astype(jnp.bfloat16),
        sum_qkv,
        sum_out,
        sum_gain,
        sum_mix_attn,
        sum_mix_mlp,
        sum_up,
        sum_gate,
        sum_down,
        sum_scale_up,
        sum_scale_gate,
        stream_rms,
    )


def solution(mesh):
    return jax.shard_map(
        local,
        mesh=mesh,
        in_specs=(
            P(("dp", "tensor"), None),
            P(("dp", "tensor"), None),
            P(),
            P(("dp", "tensor"), None),
            P(("dp", "tensor"), None),
            P(("dp", "tensor")),
            P(("dp", "tensor")),
            P(("dp", "tensor")),
            P("dp", "tensor"),
            P("dp", "tensor"),
            P("dp", "tensor"),
            P("tensor"),
            P("tensor"),
        ),
        out_specs=(
            P(("dp", "tensor"), None),
            P(("dp", "tensor"), None),
            P(("dp", "tensor"), None),
            P(("dp", "tensor"), None),
            P(("dp", "tensor")),
            P(("dp", "tensor")),
            P(("dp", "tensor")),
            P("dp", "tensor"),
            P("dp", "tensor"),
            P("dp", "tensor"),
            P("tensor"),
            P("tensor"),
            P(),
        ),
        check_vma=False,
    )
```

profile of v0, /device:TPU:0, one launch (start us, length us, event | category | flops | bytes accessed | tf_op | source)
XLA Modules:
  0.0 1130.8 jit_solution(18444926641798462416)
XLA Ops:
  10.5 43.1 %all-reduce.8 = (bf16[1024]{0:T(1024)(128)(2,1)S(1)}, bf16[1024]{0:T(1024)(128)(2,1)S(1)}, bf16[1024]{0:T(1024)(128)(2,1)S(1)}) all-reduce(bf16[1024]{0:T(1024)(128)(2,1)S(1)} %dynamic-update-slice.1, bf16[1024]{0:T(1024)(128)(2,1)S(1)} %dynamic-update-slice, ...), channel_id=1, replica_groups=mesh['dp'=8,'tensor'=4] {'dp','tensor'}, use_global_device_ids=true, to_apply=%add.1 | all-reduce | flops 3072 | bytes 12288
  53.6 29.8 %all-gather.10.cloned.1.call-done = bf16[1024,3072]{1,0:T(8,128)(2,1)} async-done(((bf16[32,3072]{1,0:T(8,128)(2,1)}), bf16[1024,3072]{1,0:T(8,128)(2,1)}) %all-gather.10.cloned.1.call-update) | async-done | bytes 6291472 | tf_op jit(solution)/shard_map/all_gather | solution.py:69
  83.4 4.8 fusion.94
  106.9 15.3 %all-gather.14.cloned.1.call-done = bf16[1024,1024]{1,0:T(8,128)(2,1)} async-done(((bf16[256,1024]{1,0:T(8,128)(2,1)}), bf16[1024,1024]{1,0:T(8,128)(2,1)}) %all-gather.14.cloned.1.call-update) | async-done | bytes 2097168 | tf_op jit(solution)/shard_map/all_gather | solution.py:104
  125.1 23.5 %while.47 = (s32[]{:T(128)}, f32[16,256]{1,0:T(8,128)S(1)}, f32[16,256]{1,0:T(8,128)S(1)}, s32[2]{0:T(128)S(1)}, s32[1024]{0:T(1024)S(1)}, /*index=5*/s32[]{:T(1...) while((s32[]{:T(128)}, f32[16,256]{1,0:T(8,128)S(1)}, ...), condition=%wide.region_5.6_spmd.clone, body=%wide.region_2.5_spmd.clone.sunk | while | flops 285496576 | bytes 21062868 | solution.py:133
  127.4 5.0 fusion.183
  139.2 4.8 fusion.183
  144.0 4.5 select_reduce_fusion.2
  152.5 20.4 %while.48 = (s32[]{:T(128)}, f32[256,16,64]{0,2,1:T(8,128)}, s32[2]{0:T(128)S(1)}, bf16[1024,1024]{0,1:T(8,128)(2,1)}, s32[1024]{0:T(1024)S(1)}, /*index=5*/s32[...) while((s32[]{:T(128)}, f32[256,16,64]{0,2,1:T(8,128)}, ...), condition=%wide.region_7.8_spmd.clone, body=%wide.region_6.7_spmd.clone.sunk | while | flops 546047232 | bytes 9200861 | solution.py:157
  157.5 5.1 fusion.189
  167.5 5.4 fusion.189
  174.2 31.9 %all-gather.16.cloned.1.call-done = bf16[1024,1024]{1,0:T(8,128)(2,1)} async-done(((bf16[32,1024]{1,0:T(8,128)(2,1)}), bf16[1024,1024]{1,0:T(8,128)(2,1)}) %all-gather.16.cloned.1.call-update) | async-done | bytes 2097168 | tf_op jit(solution)/shard_map/all_gather | solution.py:70
  214.7 41.5 %all-gather.22.cloned.1.call-done = bf16[1024,1024]{1,0:T(8,128)(2,1)} async-done(((bf16[128,1024]{1,0:T(8,128)(2,1)}), bf16[1024,1024]{1,0:T(8,128)(2,1)}) %all-gather.22.cloned.1.call-update) | async-done | bytes 2097168 | tf_op jit(solution)/shard_map/all_gather | solution.py:77
  256.3 23.1 %all-gather.18.cloned.1.call-done = bf16[1024,1024]{1,0:T(8,128)(2,1)} async-done(((bf16[256,1024]{1,0:T(8,128)(2,1)}), bf16[1024,1024]{1,0:T(8,128)(2,1)}) %all-gather.18.cloned.1.call-update) | async-done | bytes 2097168 | tf_op jit(solution)/shard_map/all_gather | solution.py:166
  279.4 6.5 fusion.95
  285.9 45.0 %all-gather.20.cloned.1.call-done = bf16[1024,1024]{1,0:T(8,128)(2,1)} async-done(((bf16[128,1024]{1,0:T(8,128)(2,1)}), bf16[1024,1024]{1,0:T(8,128)(2,1)}) %all-gather.20.cloned.1.call-update) | async-done | bytes 2097168 | tf_op jit(solution)/shard_map/all_gather | solution.py:76
  330.8 8.9 multiply_convert_fusion.2
  339.7 41.1 %all-gather.24.cloned.1.call-done = bf16[1024,1024]{1,0:T(8,128)(2,1)} async-done(((bf16[128,1024]{1,0:T(8,128)(2,1)}), bf16[1024,1024]{1,0:T(8,128)(2,1)}) %all-gather.24.cloned.1.call-update) | async-done | bytes 2097168 | tf_op jit(solution)/shard_map/all_gather | solution.py:78
  380.7 5.9 convolution_convert_fusion.3
  386.8 30.0 %reduce-scatter.11.cloned.1.call-done = bf16[256,1024]{1,0:T(8,128)(2,1)} async-done(((bf16[1024,1024]{1,0:T(8,128)(2,1)}), bf16[256,1024]{1,0:T(8,128)(2,1)}) %reduce-scatter.11.cloned.1.call-update) | async-done | bytes 524304 | tf_op jit(solution)/shard_map/reduce_scatter | solution.py:174
  426.6 22.5 %all-gather.26.cloned.1.call-done = bf16[1024,1024]{1,0:T(8,128)(2,1)} async-done(((bf16[256,1024]{1,0:T(8,128)(2,1)}), bf16[1024,1024]{1,0:T(8,128)(2,1)}) %all-gather.26.cloned.1.call-update) | async-done | bytes 2097168 | tf_op jit(solution)/shard_map/all_gather | solution.py:192
  449.1 9.7 multiply_reduce_fusion
  466.1 31.1 %reduce-scatter.13.cloned.1.call-done = bf16[256,1024]{1,0:T(8,128)(2,1)} async-done(((bf16[1024,1024]{1,0:T(8,128)(2,1)}), bf16[256,1024]{1,0:T(8,128)(2,1)}) %reduce-scatter.13.cloned.1.call-update) | async-done | bytes 524304 | tf_op jit(solution)/shard_map/reduce_scatter | solution.py:206
  510.0 48.2 %while.46 = (s32[]{:T(128)}, bf16[2,512,2048]{1,2,0:T(8,128)(2,1)}, s32[2]{0:T(128)S(1)}, s32[1024]{0:T(1024)S(1)}, s32[]{:T(128)}, /*index=5*/bf16[1024,1024]{0...) while((s32[]{:T(128)}, bf16[2,512,2048]{1,2,0:T(8,128)(2,1)}, ...), condition=%wide.region_23.24_spmd.clone, body=%wide.region_22.23_spmd.clone.sunk | while | flops 1100219648 | bytes 44492540 | solution.py:277
  514.6 4.6 fusion.177
  519.2 8.3 fusion.179
  527.5 5.2 fusion.178
  538.8 4.6 fusion.177
  543.3 8.3 fusion.179
  551.6 5.2 fusion.178
  558.2 6.5 copy.85
  564.8 5.9 convolution_convert_fusion
  571.0 7.6 convolution_convert_fusion.1
  578.6 6.0 convolution_convert_fusion.2
  589.4 35.1 %while.49 = (s32[]{:T(128)}, f32[256,16,64]{0,2,1:T(8,128)}, s32[2]{0:T(128)S(1)}, bf16[1024,1024]{0,1:T(8,128)(2,1)S(1)}, s32[1024]{0:T(1024)S(1)}, /*index=5*/...) while((s32[]{:T(128)}, f32[256,16,64]{0,2,1:T(8,128)}, ...), condition=%wide.region_20.21_spmd.clone, body=%wide.region_19.20_spmd.clone.sunk | while | flops 818676992 | bytes 31761672 | solution.py:252
  594.0 4.6 fusion.196
  598.6 8.3 fusion.197
  611.5 4.6 fusion.196
  616.0 8.5 fusion.197
  645.1 6.4 convolution_bitcast_fusion
  651.4 12.7 %copy.96 = f32[1024,3072]{1,0:T(8,128)} copy(f32[1024,3072]{0,1:T(8,128)} %convolution_bitcast_fusion) | data formatting | bytes 25165824
  664.8 22.2 %all-reduce.7 = (f32[1024]{0:T(1024)}, f32[1024]{0:T(1024)}) all-reduce(f32[1024]{0:T(1024)S(1)} %copy-done.45, f32[1024]{0:T(1024)S(1)} %copy-done.44), channel_id=1, replica_groups=mesh['dp'=8,'tensor'=4] {'dp'}, use_global_device_ids=true, to_apply=%region_38.39 | all-reduce | flops 2048 | bytes 16384 | tf_op jit(solution)/shard_map/psum | solution.py:317
  688.8 62.9 %reduce-scatter.21.cloned.1.call-done = bf16[128,1024]{1,0:T(8,128)(2,1)} async-done(((bf16[1024,1024]{1,0:T(8,128)(2,1)}), bf16[128,1024]{1,0:T(8,128)(2,1)}) %reduce-scatter.21.cloned.1.call-update) | async-done | bytes 262160 | tf_op jit(solution)/shard_map/reduce_scatter | solution.py:310
  753.5 68.8 %reduce-scatter.19.cloned.1.call-done = bf16[128,1024]{1,0:T(8,128)(2,1)} async-done(((bf16[1024,1024]{1,0:T(8,128)(2,1)}), bf16[128,1024]{1,0:T(8,128)(2,1)}) %reduce-scatter.19.cloned.1.call-update) | async-done | bytes 262160 | tf_op jit(solution)/shard_map/reduce_scatter | solution.py:307
  826.1 41.0 %all-reduce.6 = (f32[1024]{0:T(1024)S(1)}, f32[1024]{0:T(1024)S(1)}, f32[1024]{0:T(1024)S(1)}, f32[3]{0:T(128)S(1)}) all-reduce(f32[1024]{0:T(1024)S(1)} %get-tuple-element.670, f32[1024]{0:T(1024)S(1)} %copy-done.39, f32[1024]{0:T(1024)S(1)} %copy-done.38, ...), channel_id=7, replica_groups=mesh['dp'=8,'tensor'=4] {'dp','tensor'}, use_global_device_ids=true, to_apply=%region_29.30.clone | all-reduce | flops 3075 | bytes 24600
  869.3 5.4 fusion.68
  874.8 90.5 %reduce-scatter.17.cloned.1.call-done = f32[32,1024]{1,0:T(8,128)} async-done(((f32[1024,1024]{1,0:T(8,128)}), f32[32,1024]{1,0:T(8,128)}) %reduce-scatter.17.cloned.1.call-update) | async-done | bytes 131088 | tf_op jit(solution)/shard_map/reduce_scatter | solution.py:301
  965.2 158.8 %reduce-scatter.25.cloned.1.call-done = f32[32,3072]{1,0:T(8,128)} async-done(((f32[1024,3072]{1,0:T(8,128)}), f32[32,3072]{1,0:T(8,128)}) %reduce-scatter.25.cloned.1.call-update) | async-done | bytes 393232
  (293 shorter events, 139.3 us)
Async XLA Ops:
  7.2 76.2 %all-gather.10.cloned.1.call-start = ((), (), s32[]{:S(2)}) async-start(), calls=%async_computation.8 | async-start | bytes 6488064 | tf_op jit(solution)/shard_map/all_gather | solution.py:69
  7.9 114.3 %all-gather.14.cloned.1.call-start = ((), (), s32[]{:S(2)}) async-start(), calls=%async_computation.10 | async-start | bytes 2621440 | tf_op jit(solution)/shard_map/all_gather | solution.py:104
  53.6 34.6 %copy-start.42 = (bf16[1024]{0:T(1024)(128)(2,1)}, bf16[1024]{0:T(1024)(128)(2,1)S(1)}, u32[]{:S(2)}) copy-start(bf16[1024]{0:T(1024)(128)(2,1)S(1)} %get-tuple-element.650) | copy-start | bytes 6148
  53.6 52.0 %copy-start.40 = (bf16[1024]{0:T(1024)(128)(2,1)}, bf16[1024]{0:T(1024)(128)(2,1)S(1)}, u32[]{:S(2)}) copy-start(bf16[1024]{0:T(1024)(128)(2,1)S(1)} %get-tuple-element.651) | copy-start | bytes 6148
  53.6 43.9 %copy-start.36 = (f32[1024]{0:T(1024)}, f32[1024]{0:T(1024)S(1)}, u32[]{:S(2)}) copy-start(f32[1024]{0:T(1024)S(1)} %convert_element_type.116) | copy-start | bytes 12292
  92.6 8.3 copy-start.10
  94.6 6.4 copy-start.17
  97.5 9.4 copy-start.12
  97.5 7.4 copy-start.50
  100.9 47.6 %all-gather.12.cloned.1.call-start = ((), (), s32[]{:S(2)}) async-start(), calls=%async_computation.9 | async-start | bytes 2621440 | tf_op jit(solution)/shard_map/all_gather | solution.py:105
  103.1 103.0 %all-gather.16.cloned.1.call-start = ((), (), s32[]{:S(2)}) async-start(), calls=%async_computation.11 | async-start | bytes 2162688 | tf_op jit(solution)/shard_map/all_gather | solution.py:70
  103.7 152.6 %all-gather.22.cloned.1.call-start = ((), (), s32[]{:S(2)}) async-start(), calls=%async_computation.14 | async-start | bytes 2359296 | tf_op jit(solution)/shard_map/all_gather | solution.py:77
  104.3 175.1 %all-gather.18.cloned.1.call-start = ((), (), s32[]{:S(2)}) async-start(), calls=%async_computation.12 | async-start | bytes 2621440 | tf_op jit(solution)/shard_map/all_gather | solution.py:166
  174.2 38.8 %copy-start.14 = (bf16[256,16,64]{0,2,1:T(8,128)(2,1)}, bf16[256,16,64]{0,2,1:T(8,128)(2,1)S(1)}, u32[]{:S(2)}) copy-start(bf16[256,16,64]{0,2,1:T(8,128)(2,1)S(1)} %convert_element_type.119) | copy-start | bytes 1572868
  206.1 8.6 copy-start.46
  206.1 8.6 copy-start.47
  213.0 117.8 %all-gather.20.cloned.1.call-start = ((), (), s32[]{:S(2)}) async-start(), calls=%async_computation.13 | async-start | bytes 2359296 | tf_op jit(solution)/shard_map/all_gather | solution.py:76
  213.7 167.0 %all-gather.24.cloned.1.call-start = ((), (), s32[]{:S(2)}) async-start(), calls=%async_computation.15 | async-start | bytes 2359296 | tf_op jit(solution)/shard_map/all_gather | solution.py:78
  214.5 202.3 %reduce-scatter.11.cloned.1.call-start = ((), (), s32[]{:S(2)}) async-start(), calls=%async_computation.16 | async-start | bytes 2621440 | tf_op jit(solution)/shard_map/reduce_scatter | solution.py:174
  386.7 62.4 %all-gather.26.cloned.1.call-start = ((), (), s32[]{:S(2)}) async-start(), calls=%async_computation.17 | async-start | bytes 2621440 | tf_op jit(solution)/shard_map/all_gather | solution.py:192
  416.8 5.1 copy-start.7
  426.3 71.0 %reduce-scatter.13.cloned.1.call-start = ((), (), s32[]{:S(2)}) async-start(), calls=%async_computation.18 | async-start | bytes 2621440 | tf_op jit(solution)/shard_map/reduce_scatter | solution.py:206
  449.1 9.7 copy-start.49
  465.7 164.9 %reduce-scatter.15.cloned.1.call-start = ((), (), s32[]{:S(2)}) async-start(), calls=%async_computation.19 | async-start | bytes 5242880 | tf_op jit(solution)/shard_map/reduce_scatter | solution.py:278
  497.3 6.7 copy-start.5
  500.2 5.5 copy-start.29
  527.4 5.2 copy-start.1
  551.6 5.2 copy-start.1
  558.2 6.5 copy-start.23
  564.7 122.3 %reduce-scatter.23.cloned.1.call-start = ((), (), s32[]{:S(2)}) async-start(), calls=%async_computation.23 | async-start | bytes 2359296 | tf_op jit(solution)/shard_map/reduce_scatter | solution.py:313
  570.7 181.0 %reduce-scatter.21.cloned.1.call-start = ((), (), s32[]{:S(2)}) async-start(), calls=%async_computation.22 | async-start | bytes 2359296 | tf_op jit(solution)/shard_map/reduce_scatter | solution.py:310
  578.5 6.2 copy-start.15
  578.6 243.7 %reduce-scatter.19.cloned.1.call-start = ((), (), s32[]{:S(2)}) async-start(), calls=%async_computation.21 | async-start | bytes 2359296 | tf_op jit(solution)/shard_map/reduce_scatter | solution.py:307
  584.7 380.6 %reduce-scatter.17.cloned.1.call-start = ((), (), s32[]{:S(2)}) async-start(), calls=%async_computation.20 | async-start | bytes 4325376 | tf_op jit(solution)/shard_map/reduce_scatter | solution.py:301
  588.4 535.6 %reduce-scatter.25.cloned.1.call-start = ((), (), s32[]{:S(2)}) async-start(), calls=%async_computation.24 | async-start | bytes 12976128
  624.5 6.1 copy-start.37
  627.3 8.2 copy-start.9
  627.3 8.2 copy-start.33
  632.7 8.9 copy-start.11
  632.7 8.9 copy-start.13
  640.4 4.6 copy-start.25
  645.0 6.4 copy-start.21
  664.1 162.0 %copy-start.38 = (f32[1024]{0:T(1024)S(1)}, f32[1024]{0:T(1024)}, u32[]{:S(2)}) copy-start(f32[1024]{0:T(1024)} %get-tuple-element.550) | copy-start | bytes 12292
  664.1 162.0 %copy-start.39 = (f32[1024]{0:T(1024)S(1)}, f32[1024]{0:T(1024)}, u32[]{:S(2)}) copy-start(f32[1024]{0:T(1024)} %get-tuple-element.552) | copy-start | bytes 12292
  664.1 205.2 %copy-start.20 = (f32[256,1024]{1,0:T(8,128)S(1)}, f32[256,1024]{1,0:T(8,128)}, u32[]{:S(2)}) copy-start(f32[256,1024]{1,0:T(8,128)} %copy-done.19) | copy-start | bytes 3145732
  664.1 205.2 %copy-start.22 = (bf16[256,1024]{1,0:T(8,128)(2,1)S(1)}, bf16[256,1024]{1,0:T(8,128)(2,1)}, u32[]{:S(2)}) copy-start(bf16[256,1024]{1,0:T(8,128)(2,1)} %copy-done.21) | copy-start | bytes 1572868
  664.1 205.2 %copy-start.26 = (bf16[256,1024]{1,0:T(8,128)(2,1)S(1)}, bf16[256,1024]{1,0:T(8,128)(2,1)}, u32[]{:S(2)}) copy-start(bf16[256,1024]{1,0:T(8,128)(2,1)} %copy.89) | copy-start | bytes 1572868
  664.1 205.2 %copy-start.28 = (bf16[256,1024]{1,0:T(8,128)(2,1)S(1)}, bf16[256,1024]{1,0:T(8,128)(2,1)}, u32[]{:S(2)}) copy-start(bf16[256,1024]{1,0:T(8,128)(2,1)} %copy-done.27) | copy-start | bytes 1572868
  (24 other events, 50.8 us)
Sparse Core Ops, SparseCore 0:
  10.9 72.4 all-gather.9
  101.1 21.0 all-gather.13
  124.3 22.5 all-gather.11
  149.7 56.3 all-gather.15
  208.1 48.1 all-gather.21
  258.2 21.0 all-gather.17
  281.5 49.2 all-gather.19
  332.9 47.7 all-gather.23
  386.8 29.8 reduce-scatter.10
  426.4 22.5 all-gather.25
  465.8 31.4 reduce-scatter.12
  564.9 44.4 reduce-scatter.14
  613.3 67.9 reduce-scatter.22
  685.2 66.4 reduce-scatter.20
  755.5 66.7 reduce-scatter.18
  825.1 140.0 reduce-scatter.16
  972.7 151.2 reduce-scatter.24
where the time goes:
time: 1140 us; the launch traced here: 1130 us
  waiting for transfers between devices  695 us (61%)
  matrix products  163 us (14%)
  blocking collectives  106 us (9%)
  local copies, waits for them, and re-layouts  81.6 us (7%)
  other arithmetic  62.1 us (5%)
  between operations  14.9 us (1%)
    unnamed x18, waiting for transfers between devices  162 us
    reduce_scatter x1, waiting for transfers between devices, local(): lax.psum_scatter(grad_out, ('dp', 'tensor'), scatter_dimension=0, tiled=T...  90.5 us
    unnamed x2, blocking collectives  84.1 us
    reduce_scatter x1, waiting for transfers between devices, local(): lax.psum_scatter(grad_up.astype(jnp.bfloat16), 'dp', scatter_dimension=0,...  68.8 us
    reduce_scatter x1, waiting for transfers between devices, local(): lax.psum_scatter(grad_gate.astype(jnp.bfloat16), 'dp', scatter_dimension=...  62.9 us
    all_gather x1, waiting for transfers between devices, local(): lax.all_gather(w_up, 'dp', axis=0, tiled=True)  45 us
    all_gather x1, waiting for transfers between devices, local(): lax.all_gather(w_gate, 'dp', axis=0, tiled=True)  41.5 us
    all_gather x1, waiting for transfers between devices, local(): lax.all_gather(w_down, 'dp', axis=0, tiled=True)  41.1 us
  transfers between devices with their start and end apart: 17, of which 14 were waited for; matrix products, arithmetic and copies ran while one was open for 17% of the time, Pallas kernels for 0%

commit v1 on v0

--- a/solution.py
+++ b/solution.py
@@ -1,8 +1,11 @@
+import functools
 import math
 
 import jax
 import jax.numpy as jnp
 from jax import lax
+from jax.experimental import pallas as pl
+from jax.experimental.pallas import tpu as pltpu
 from jax.sharding import PartitionSpec as P
 
 HEAD_DIM = 64
@@ -335,9 +338,769 @@
     )
 
 
+MESH = pl.DeviceIdType.MESH
+BF16 = jnp.bfloat16
+F32 = jnp.float32
+LOG2E = 1.4426950408889634
+COPIES = 192
+VMEM_BYTES = 63 * 2**20
+
+
+def nn(left, right):
+    return lax.dot_general(left, right, (((1,), (0,)), ((), ())), preferred_element_type=F32)
+
+
+def nt(left, right):
+    return lax.dot_general(left, right, (((1,), (1,)), ((), ())), preferred_element_type=F32)
+
+
+def tn(left, right):
+    return lax.dot_general(left, right, (((0,), (0,)), ((), ())), preferred_element_type=F32)
+
+
+def flip(index, bits):
+    bit = 1
+    while bit <= bits:
+        if bits & bit:
+            index = index + bit - 2 * bit * lax.rem(lax.div(index, bit), 2)
+        bit *= 2
+    return index
+
+
+def mean_rows(value):
+    return jnp.mean(value, axis=-1, keepdims=True)
+
+
+def fused_kernel(
+    tokens, cotangent, whole_row, w_qkv, w_out, small, w_up, w_gate, w_down, scale_u, scale_v,
+    layer_out, grad_tokens, grad_qkv, grad_out, grad_up, grad_gate, grad_down, stats_out,
+    tok, wq, wo, wu, wg, wd, small_t, small_d, gains,
+    raw, qkv, linv, att, ato, branch, hid, h1, ur, gr, inn,
+    part, from_core3, from_core1, from_y,
+    dr2, dr1, db, dba, dat, dao, dqkv, delta,
+    gd, x_down, x_up, x_gate, x_qkv, x_out, z_down, z_up, z_gate, z_qkv, z_out,
+    o_core3, o_core1, o_y, osum, q_sum, q_piece, stats, s_tensor, s_x, s_z,
+    send_sem, recv_sem,
+):
+    d = lax.axis_index("dp")
+    t = lax.axis_index("tensor")
+    core, ynb, diag = (d, flip(t, 1)), (d, flip(t, 2)), (d, flip(t, 3))
+    tensor_peer = {1: core, 2: ynb, 3: diag}
+    xnb = (flip(d, 1), t)
+    z_peer = {m: (flip(d, m), t) for m in (2, 4, 6)}
+
+    barrier = pltpu.get_barrier_semaphore()
+    peers = [core, ynb, diag, xnb] + [z_peer[m] for m in (2, 4, 6)]
+    for peer in peers:
+        pl.semaphore_signal(barrier, inc=1, device_id=peer, device_id_type=MESH)
+    pl.semaphore_wait(barrier, len(peers))
+
+    issued = []
+
+    def send(src, dst, peer):
+        index = len(issued)
+        copy = pltpu.make_async_remote_copy(
+            src_ref=src,
+            dst_ref=dst,
+            send_sem=send_sem.at[index],
+            recv_sem=recv_sem.at[index],
+            device_id=peer,
+            device_id_type=MESH,
+        )
+        copy.start()
+        issued.append(copy)
+        return copy
+
+    waited = set()
+
+    def sent(copy):
+        if id(copy) not in waited:
+            waited.add(id(copy))
+            copy.wait_send()
+
+    def rows(start, count=256):
+        return pl.ds(pl.multiple_of(start * count, count), count)
+
+    def block(r):
+        return pl.ds(r * 256, 256)
+
+    class Gather:
+        def __init__(self, src, view):
+            self.src, self.view = src, view
+
+        def start(self):
+            own = self.view(d)
+            self.z = {m: send(self.src, own, z_peer[m]) for m in (2, 4, 6)}
+            self.x = [send(self.src, own, xnb)]
+
+        def forward(self):
+            for m in (2, 4, 6):
+                self.z[m].wait_recv()
+                part_ref = self.view(flip(d, m))
+                self.x.append(send(part_ref, part_ref, xnb))
+
+        def finish(self):
+            for copy in self.x:
+                copy.wait_recv()
+
+    def rows_of(ref):
+        return lambda index: ref.at[pl.ds(pl.multiple_of(index * 128, 128), 128)]
+
+    take_qkv = Gather(
+        wq.at[:, pl.ds(pl.multiple_of(d * 128, 128), 128), :],
+        lambda index: wq.at[:, pl.ds(pl.multiple_of(index * 128, 128), 128), :],
+    )
+    take_small = Gather(small_d.at[d], lambda index: small_d.at[index])
+    take_out = Gather(w_out, lambda index: wo.at[index, t])
+    take_up = Gather(w_up, rows_of(wu))
+    take_gate = Gather(w_gate, rows_of(wg))
+    take_down = Gather(w_down, rows_of(wd))
+
+    qkv_own = pl.ds(pl.multiple_of(d * 128 + t * 32, 32), 32)
+    qkv_sends = [
+        send(
+            w_qkv.at[:, :, pl.ds(pl.multiple_of(flip(t, r) * 256, 256), 256)],
+            wq.at[:, qkv_own, :],
+            tensor_peer[r],
+        )
+        for r in (1, 2, 3)
+    ]
+    small_sends = [send(small, small_t.at[r - 1], tensor_peer[r]) for r in (1, 2, 3)]
+    tok_y = send(tokens, tok.at[block(2)], ynb)
+    tok_core = send(tokens, tok.at[block(1)], core)
+    tok[0:256, :] = tokens[...]
+    wq[:, qkv_own, :] = w_qkv[:, :, pl.ds(pl.multiple_of(t * 256, 256), 256)]
+    wo[d, t] = w_out[...]
+    wu[pl.ds(pl.multiple_of(d * 128, 128), 128), :] = w_up[...]
+    wg[pl.ds(pl.multiple_of(d * 128, 128), 128), :] = w_gate[...]
+    wd[pl.ds(pl.multiple_of(d * 128, 128), 128), :] = w_down[...]
+    stats[...] = jnp.zeros_like(stats)
+    for copy in small_sends:
+        copy.wait_recv()
+    small_d[d] = small[...] + small_t[0] + small_t[1] + small_t[2]
+    take_small.start()
+    for copy in qkv_sends:
+        copy.wait_recv()
+    take_qkv.start()
+
+    take_small.forward()
+    take_qkv.forward()
+    take_out.start()
+    take_up.start()
+    tok_y.wait_recv()
+    tok_diag = send(tok.at[block(2)], tok.at[block(3)], core)
+    take_small.finish()
+    total = small_d[0].astype(F32)
+    for index in range(1, 8):
+        total = total + small_d[index].astype(F32)
+    gains[...] = total
+    take_qkv.finish()
+    tok_core.wait_recv()
+    tok_diag.wait_recv()
+
+    head_col = pl.ds(pl.multiple_of(t * 256, 256), 256)
+    gain_qk = gains[0:1, head_col]
+    lane = lax.broadcasted_iota(jnp.int32, (1, 256), 1)
+    lane_head = lax.div(lane, HEAD_DIM)
+    same_head = jnp.where(
+        lax.div(lax.broadcasted_iota(jnp.int32, (256, 256), 0), HEAD_DIM)
+        == lax.div(lax.broadcasted_iota(jnp.int32, (256, 256), 1), HEAD_DIM),
+        1.0,
+        0.0,
+    ).astype(BF16)
+
+    def head_sum(value):
+        high = value.astype(BF16)
+        low = (value - high.astype(F32)).astype(BF16)
+        return nn(high, same_head) + nn(low, same_head)
+
+    def qkv_step(r, carry):
+        at = rows(r)
+        x = tok[at, :]
+        for j in range(3):
+            y = nn(x, wq[j])
+            if j < 2:
+                raw[j, at, :] = y
+                factor = lax.rsqrt(head_sum(y * y) + EPSILON)
+                qkv[j, at, :] = (y * factor * gain_qk).astype(BF16)
+            else:
+                qkv[j, at, :] = y.astype(BF16)
+        return carry
+
+    lax.fori_loop(0, 4, qkv_step, 0)
+    take_out.forward()
+    take_gate.start()
+
+    def true_rows(i):
+        return rows(flip(t, i))
+
+    whole = whole_row[...]
+    row_id = lax.broadcasted_iota(jnp.int32, (256, 256), 0)
+    col_id = lax.broadcasted_iota(jnp.int32, (256, 256), 1)
+    exp_scale = math.sqrt(HEAD_DIM) * LOG2E
+
+    def attend(i):
+        at = true_rows(i)
+
+        def head_step(h, carry):
+            mask = lane_head == h
+            q = jnp.where(mask, qkv[0, at, :], 0).astype(BF16)
+            acc = jnp.zeros((256, 256), F32)
+            weight = jnp.zeros((256, 1), F32)
+            for j in range(i + 1):
+                key_at = true_rows(j)
+                e = jnp.exp2(nt(q, qkv[1, key_at, :]) * exp_scale)
+                if j == i:
+                    e = jnp.where(col_id <= row_id, e, 0.0)
+                elif j // 2 != i // 2:
+                    e = e * whole
+                weight = weight + jnp.sum(e, axis=1, keepdims=True)
+                acc = acc + nn(e.astype(BF16), qkv[2, key_at, :])
+            inverse = 1.0 / weight
+            linv[at, :] = jnp.where(mask, inverse, linv[at, :])
+            att[at, :] = jnp.where(mask, (acc * inverse).astype(BF16), att[at, :])
+            return carry
+
+        linv[at, :] = jnp.zeros((256, 256), F32)
+        att[at, :] = jnp.zeros((256, 256), BF16)
+        lax.fori_loop(0, 4, head_step, 0)
+
+    attend(0)
+    attend(1)
+    attend(2)
+    take_up.forward()
+    take_down.start()
+    attend(3)
+
+    att_sends = [send(att.at[block(r)], ato.at[t], tensor_peer[r]) for r in (2, 3, 1)]
+    ato[t] = att[block(0), :]
+    take_out.finish()
+    wo_y = send(wo.at[:, t], wo.at[:, t], ynb)
+    wo_core = send(wo.at[:, t], wo.at[:, t], core)
+    wo_y.wait_recv()
+    wo_far = send(wo.at[:, flip(t, 2)], wo.at[:, flip(t, 2)], core)
+    for copy in att_sends:
+        copy.wait_recv()
+    wo_core.wait_recv()
+    wo_far.wait_recv()
+
+    def out_rows(slot, columns):
+        return wo[2 * slot : 2 * slot + 2, :, :, columns].reshape(256, 256)
+
+    def out_step(n, carry):
+        at = rows(n)
+        acc = nn(ato[0], out_rows(0, at))
+        for slot in range(1, 4):
+            acc = acc + nn(ato[slot], out_rows(slot, at))
+        branch[:, at] = acc
+        return carry
+
+    lax.fori_loop(0, 4, out_step, 0)
+
+    mix_a = gains[1:2, :]
+    mix_m = gains[2:3, :]
+    CH = 32
+
+    def add_stat(row, value):
+        stats[row : row + 1, :] = stats[row : row + 1, :] + jnp.sum(value, axis=0, keepdims=True)
+
+    def first_norm(at):
+        x = tokens[at, :].astype(F32)
+        ba = branch[at, :]
+        fa = lax.rsqrt(mean_rows(ba * ba) + EPSILON)
+        ha = ba * fa
+        r1 = x + mix_a * (ha - x)
+        f1 = lax.rsqrt(mean_rows(r1 * r1) + EPSILON)
+        return x, ba, fa, ha, f1, r1 * f1
+
+    def norm_step(c, carry):
+        at = rows(c, CH)
+        _, ba, _, _, _, hidden = first_norm(at)
+        add_stat(3, ba * ba)
+        hid[at, :] = hidden
+        h1[at, :] = hidden.astype(BF16)
+        return carry
+
+    lax.fori_loop(0, 256 // CH, norm_step, 0)
+
+    def spread(ref):
+        return send(ref.at[block(0)], ref.at[block(2)], ynb), send(
+            ref.at[block(0)], ref.at[block(1)], core
+        )
+
+    def relay(ref, from_ynb):
+        from_ynb.wait_recv()
+        return send(ref.at[block(2)], ref.at[block(3)], core)
+
+    h1_y, h1_core = spread(h1)
+    h1_far = relay(h1, h1_y)
+    take_gate.forward()
+    take_down.forward()
+    take_up.finish()
+    take_gate.finish()
+    h1_core.wait_recv()
+    h1_far.wait_recv()
+
+    def up_step(index, carry):
+        f = lax.rem(index, 4)
+        at, cols = rows(lax.div(index, 4)), rows(f)
+        hidden = h1[at, :]
+        u_raw = nn(hidden, wu[:, cols])
+        g_raw = nn(hidden, wg[:, cols])
+        gate = g_raw * scale_v[:, cols]
+        silu = gate / (1.0 + jnp.exp(-gate))
+        ur[at, cols] = u_raw.astype(BF16)
+        gr[at, cols] = g_raw.astype(BF16)
+        inn[at, cols] = (u_raw * scale_u[:, cols] * silu).astype(BF16)
+        return carry
+
+    lax.fori_loop(0, 16, up_step, 0)
+    take_down.finish()
+
+    class Reduce:
+        def __init__(self, which, before, make):
+            self.which, self.before, self.make = which, before, make
+
+        def run(self):
+            k = self.which
+            waits = self.before.copies if self.before else {}
+            self.copies = {}
+            for r in (3, 2, 1, 0):
+                if r in waits:
+                    sent(waits[r])
+                self.make(r)
+                if r == 3:
+                    self.copies[3] = send(part.at[block(3)], from_core3.at[k], core)
+                elif r == 2:
+                    self.copies[3].wait_recv()
+                    part[block(2), :] = (
+                        part[block(2), :].astype(F32) + from_core3[k].astype(F32)
+                    ).astype(BF16)
+                    self.copies[2] = send(part.at[block(2)], from_y.at[k], ynb)
+                elif r == 1:
+                    self.copies[1] = send(part.at[block(1)], from_core1.at[k], core)
+
+        def finish(self):
+            self.copies[1].wait_recv()
+            self.copies[2].wait_recv()
+
+        def at(self, where):
+            k = self.which
+            return (
+                part[where, :].astype(F32)
+                + from_core1[k, where, :].astype(F32)
+                + from_y[k, where, :].astype(F32)
+            )
+
+    def make_down(r):
+        def step(n, carry):
+            cols = rows(n)
+            part[block(r), cols] = nt(inn[block(r), :], wd[cols, :]).astype(BF16)
+            return carry
+
+        lax.fori_loop(0, 4, step, 0)
+
+    sum_m = Reduce(0, None, make_down)
+    sum_m.run()
+    sum_m.finish()
+
+    def loss_step(c, carry):
+        at = rows(c, CH)
+        bm = sum_m.at(at)
+        hidden = hid[at, :]
+        fm = lax.rsqrt(mean_rows(bm * bm) + EPSILON)
+        hm = bm * fm
+        r2 = hidden + mix_m * (hm - hidden)
+        f2 = lax.rsqrt(mean_rows(r2 * r2) + EPSILON)
+        result = r2 * f2
+        layer_out[at, :] = result.astype(BF16)
+        up = cotangent[at, :].astype(F32)
+        grad = f2 * (up - result * mean_rows(up * result))
+        dr2[at, :] = grad
+        add_stat(1, grad * (hm - hidden))
+        add_stat(4, bm * bm)
+        add_stat(5, r2 * r2)
+        c_m = mix_m * grad
+        db[at, :] = (fm * (c_m - hm * mean_rows(c_m * hm))).astype(BF16)
+        return carry
+
+    lax.fori_loop(0, 256 // CH, loss_step, 0)
+
+    class Scatter:
+        def __init__(self, view, from_x, from_z):
+            self.view, self.from_x, self.from_z = view, from_x, from_z
+            self.x, self.z = {}, {}
+
+        def ship(self, k):
+            self.x[k] = send(self.view(flip(d, 2 * k + 1)), self.from_x.at[k], xnb)
+
+        def fold(self, k):
+            self.x[k].wait_recv()
+            own = self.view(flip(d, 2 * k))
+            own[...] = (own[...].astype(F32) + self.from_x[k].astype(F32)).astype(BF16)
+            if k:
+                self.z[k] = send(own, self.from_z.at[k - 1], z_peer[2 * k])
+
+        def total(self):
+            for k in (3, 2, 1):
+                self.z[k].wait_recv()
+            own = self.view(d)[...].astype(F32)
+            for k in range(3):
+                own = own + self.from_z[k].astype(F32)
+            return own
+
+    def release(gather):
+        for copy in [*gather.z.values(), *gather.x]:
+            sent(copy)
+
+    def weight_grad(left, right, out, scatter):
+        for k in (3, 2, 1, 0):
+            at = rows(lax.div(flip(d, 2 * k), 2))
+
+            def step(n, carry):
+                cols = rows(n)
+                out[at, cols] = tn(left[:, at], right[:, cols]).astype(BF16)
+                return carry
+
+            lax.fori_loop(0, 4, step, 0)
+            scatter.ship(k)
+
+    db_y, db_core = spread(db)
+    db_far = relay(db, db_y)
+    db_core.wait_recv()
+    db_far.wait_recv()
+
+    sum_down = Scatter(rows_of(gd), x_down, z_down)
+    weight_grad(db, inn, gd, sum_down)
+
+    def make_hidden(r):
+        at = block(r)
+
+        def inner_step(f, carry):
+            cols = rows(f)
+            d_inner = nn(db[at, :], wd[:, cols])
+            u_raw = ur[at, cols].astype(F32)
+            g_raw = gr[at, cols].astype(F32)
+            gate = g_raw * scale_v[:, cols]
+            sig = 1.0 / (1.0 + jnp.exp(-gate))
+            up = u_raw * scale_u[:, cols]
+            d_up = d_inner * (gate * sig)
+            d_gate = d_inner * up * (sig * (1.0 + gate * (1.0 - sig)))
+            stats[6:7, cols] = stats[6:7, cols] + jnp.sum(d_up * u_raw, axis=0, keepdims=True)
+            stats[7:8, cols] = stats[7:8, cols] + jnp.sum(d_gate * g_raw, axis=0, keepdims=True)
+            ur[at, cols] = (d_up * scale_u[:, cols]).astype(BF16)
+            gr[at, cols] = (d_gate * scale_v[:, cols]).astype(BF16)
+            return carry
+
+        def back_step(n, carry):
+            cols = rows(n)
+            part[at, cols] = (nt(ur[at, :], wu[cols, :]) + nt(gr[at, :], wg[cols, :])).astype(BF16)
+            return carry
+
+        lax.fori_loop(0, 4, inner_step, 0)
+        lax.fori_loop(0, 4, back_step, 0)
+
+    sum_h = Reduce(1, sum_m, make_hidden)
+    sum_h.run()
+
+    gu, gg, go = wd, wu, wg
+    for gather in (take_down, take_up, take_gate):
+        release(gather)
+    sum_up = Scatter(rows_of(gu), x_up, z_up)
+    sum_gate = Scatter(rows_of(gg), x_gate, z_gate)
+    weight_grad(h1, ur, gu, sum_up)
+    sum_down.fold(3)
+    sum_down.fold(2)
+    weight_grad(h1, gr, gg, sum_gate)
+    sum_down.fold(1)
+    sum_down.fold(0)
+    sum_h.finish()
+
+    def mid_step(c, carry):
+        at = rows(c, CH)
+        x, _, fa, ha, f1, hidden = first_norm(at)
+        d_hidden = (1.0 - mix_m) * dr2[at, :] + sum_h.at(at)
+        grad = f1 * (d_hidden - hidden * mean_rows(d_hidden * hidden))
+        dr1[at, :] = grad
+        add_stat(0, grad * (ha - x))
+        c_a = mix_a * grad
+        dba[at, :] = (fa * (c_a - ha * mean_rows(c_a * ha))).astype(BF16)
+        return carry
+
+    lax.fori_loop(0, 256 // CH, mid_step, 0)
+
+    dat_sends = []
+    for r in (2, 3, 1, 0):
+        slot = flip(t, r)
+        weight = wo[pl.ds(2 * slot, 2)].reshape(256, 1024)
+        piece = nt(dba[...], weight).astype(BF16)
+        if r:
+            dat[r - 1] = piece
+            dat_sends.append(send(dat.at[r - 1], dao.at[block(r)], tensor_peer[r]))
+        else:
+            dao[block(0), :] = piece
+
+    def out_grad_step(n, carry):
+        cols = rows(n)
+        for slot in range(4):
+            g = tn(ato[slot], dba[:, cols]).astype(BF16)
+            for q in range(8):
+                start = (q % 4) * 256 + (2 * slot + q // 4) * 32
+                go[start : start + 32, cols] = g[q * 32 : (q + 1) * 32, :]
+        return carry
+
+    lax.fori_loop(0, 4, out_grad_step, 0)
+
+    def go_rows(r):
+        return rows(flip(t, r))
+
+    go_core3 = send(go.at[go_rows(3)], o_core3, core)
+    go_core1 = send(go.at[go_rows(1)], o_core1, core)
+    sum_up.fold(3)
+    sum_up.fold(2)
+    go_core3.wait_recv()
+    go[go_rows(2), :] = (go[go_rows(2), :].astype(F32) + o_core3[...].astype(F32)).astype(BF16)
+    go_y = send(go.at[go_rows(2)], o_y, ynb)
+    for copy in dat_sends:
+        copy.wait_recv()
+
+    head_rows = jnp.where(
+        lax.broadcasted_iota(jnp.int32, (8, 256), 0)
+        == lax.div(lax.broadcasted_iota(jnp.int32, (8, 256), 1), HEAD_DIM),
+        1.0,
+        0.0,
+    ).astype(BF16)
+    for copy in att_sends:
+        sent(copy)
+
+    def ready_step(r, carry):
+        at = rows(r)
+        scaled = (dao[at, :].astype(F32) * linv[at, :]).astype(BF16)
+        dao[at, :] = scaled
+        product = scaled.astype(F32) * att[at, :].astype(F32)
+        high = product.astype(BF16)
+        low = (product - high.astype(F32)).astype(BF16)
+        delta[r] = nt(head_rows, high) + nt(head_rows, low)
+        att[at, :] = qkv[1, at, :].T
+        return carry
+
+    lax.fori_loop(0, 4, ready_step, 0)
+    d_key, d_value, d_query_t = branch, hid, dr2
+    d_key[...] = jnp.zeros_like(d_key)
+    d_value[...] = jnp.zeros_like(d_value)
+    d_query_t[...] = jnp.zeros_like(d_query_t)
+
+    def attend_back(j, i):
+        key_at, query_at = true_rows(j), true_rows(i)
+        key_cols, query_cols = slice(j * 256, j * 256 + 256), slice(i * 256, i * 256 + 256)
+
+        def head_step(h, carry):
+            mask = lane_head == h
+            q = jnp.where(mask, qkv[0, query_at, :], 0).astype(BF16)
+            do = jnp.where(mask, dao[query_at, :], 0).astype(BF16)
+            e = jnp.exp2(nt(qkv[1, key_at, :], q) * exp_scale)
+            if i == j:
+                e = jnp.where(row_id <= col_id, e, 0.0)
+            elif j // 2 != i // 2:
+                e = e * whole
+            d_prob = nt(qkv[2, key_at, :], do)
+            d_score = (e * (d_prob - delta[flip(t, i), pl.ds(h, 1), :])).astype(BF16)
+            d_key[:, key_cols] += nn(d_score, q)
+            d_value[:, key_cols] += nn(e.astype(BF16), do)
+            part_rows = pl.ds(pl.multiple_of(h * HEAD_DIM, HEAD_DIM), HEAD_DIM)
+            key_t = att[pl.ds(pl.multiple_of(flip(t, j) * 256 + h * HEAD_DIM, HEAD_DIM), HEAD_DIM), :]
+            d_query_t[part_rows, query_cols] += nn(key_t, d_score)
+            return carry
+
+        lax.fori_loop(0, 4, head_step, 0)
+
+    attend_back(0, 0)
+    attend_back(0, 1)
+    sum_up.fold(1)
+    sum_up.fold(0)
+    attend_back(0, 2)
+    attend_back(0, 3)
+    sum_gate.fold(3)
+    sum_gate.fold(2)
+    attend_back(1, 1)
+    attend_back(1, 2)
+    attend_back(1, 3)
+    sum_gate.fold(1)
+    sum_gate.fold(0)
+    go_core1.wait_recv()
+    go_y.wait_recv()
+    osum[...] = (
+        go[go_rows(0), :].astype(F32) + o_core1[...].astype(F32) + o_y[...].astype(F32)
+    ).astype(BF16)
+    sum_out = Scatter(
+        lambda index: osum.at[pl.ds(pl.multiple_of(index * 32, 32), 32)], x_out, z_out
+    )
+    for k in (3, 2, 1, 0):
+        sum_out.ship(k)
+    attend_back(2, 2)
+    attend_back(2, 3)
+    attend_back(3, 3)
+
+    def qkv_back(i):
+        at = true_rows(i)
+        cols = slice(i * 256, i * 256 + 256)
+        scale = math.sqrt(HEAD_DIM)
+        for j, grad in ((0, d_query_t[:, cols].T * scale), (1, d_key[:, cols] * scale)):
+            y = raw[j, at, :]
+            factor = lax.rsqrt(head_sum(y * y) + EPSILON)
+            w = y * factor
+            stats[2:3, head_col] = stats[2:3, head_col] + jnp.sum(grad * w, axis=0, keepdims=True)
+            c = grad * gain_qk
+            dqkv[j, at, :] = (factor * (c - w * head_sum(c * w))).astype(BF16)
+        dqkv[2, at, :] = d_value[:, cols].astype(BF16)
+
+    for i in range(4):
+        qkv_back(i)
+
+    gq = qkv
+    sum_qkv = Scatter(
+        lambda index: gq.at[:, pl.ds(pl.multiple_of(index * 128, 128), 128), :], x_qkv, z_qkv
+    )
+    for k in (3, 2, 1, 0):
+        zz = lax.div(flip(d, 2 * k), 2)
+        for j in range(3):
+            gq[j, rows(zz), :] = tn(tok[:, rows(zz)], dqkv[j]).astype(BF16)
+        sum_qkv.ship(k)
+
+    small_sends = [send(stats, s_tensor.at[r - 1], tensor_peer[r]) for r in (1, 2, 3)]
+
+    def make_tokens(r):
+        def step(n, carry):
+            cols = rows(n)
+            acc = nt(dqkv[0, block(r), :], wq[0, cols, :])
+            for j in (1, 2):
+                acc = acc + nt(dqkv[j, block(r), :], wq[j, cols, :])
+            part[block(r), cols] = acc.astype(BF16)
+            return carry
+
+        lax.fori_loop(0, 4, step, 0)
+
+    sum_t = Reduce(2, sum_h, make_tokens)
+    sum_t.run()
+
+    for k in (3, 2, 1, 0):
+        sum_out.fold(k)
+    for copy in small_sends:
+        copy.wait_recv()
+    over_tensor = s_tensor[0] + s_tensor[1] + s_tensor[2]
+    shared = lax.broadcasted_iota(jnp.int32, (8, 1024), 0) < 6
+    s_x[0] = stats[...] + jnp.where(shared, over_tensor, 0.0)
+    stat_x = send(s_x.at[0], s_x.at[1], xnb)
+    for k in (3, 2, 1, 0):
+        sum_qkv.fold(k)
+    stat_x.wait_recv()
+    s_z[0] = s_x[0] + s_x[1]
+    stat_z = [send(s_z.at[0], s_z.at[k], z_peer[2 * k]) for k in (1, 2, 3)]
+
+    grad_down[...] = sum_down.total()
+    grad_up[...] = sum_up.total()
+    grad_gate[...] = sum_gate.total()
+    grad_out[...] = sum_out.total()
+    q_sum[...] = sum_qkv.total()
+    q_sends = [
+        send(
+            q_sum.at[:, pl.ds(pl.multiple_of(flip(t, r) * 32, 32), 32), :],
+            q_piece.at[t],
+            tensor_peer[r],
+        )
+        for r in (1, 2, 3)
+    ]
+    q_piece[t] = q_sum[:, pl.ds(pl.multiple_of(t * 32, 32), 32), :]
+    sum_t.finish()
+
+    def last_step(c, carry):
+        at = rows(c, CH)
+        grad_tokens[at, :] = ((1.0 - mix_a) * dr1[at, :] + sum_t.at(at)).astype(BF16)
+        return carry
+
+    lax.fori_loop(0, 256 // CH, last_step, 0)
+    for copy in stat_z:
+        copy.wait_recv()
+    stats_out[...] = s_z[0] + s_z[1] + s_z[2] + s_z[3]
+    for copy in q_sends:
+        copy.wait_recv()
+    for slot in range(4):
+        for j in range(3):
+            grad_qkv[:, j * 1024 + slot * 256 : j * 1024 + slot * 256 + 256] = q_piece[slot, j]
+    for copy in issued:
+        sent(copy)
+
+
+def fits(mesh):
+    return dict(mesh.shape) == {"dp": 8, "tensor": 4}
+
+
+def fused(
+    tokens, cotangent, bucket_start, w_qkv, w_out, s_qk, alpha_a, alpha_m, w_up, w_gate, w_down, s_u, s_v
+):
+    n_rows, width = tokens.shape
+    d, t = lax.axis_index("dp"), lax.axis_index("tensor")
+    index = d * lax.axis_size("tensor") + t
+    piece = s_qk.shape[0]
+    starts = lax.dynamic_slice_in_dim(bucket_start, d * 4, 4)
+    whole = jnp.where(starts[0] == starts[2], 1.0, 0.0)
+    whole_row = jnp.full((1, 256), whole, F32)
+    vectors = jnp.stack([s_qk, alpha_a, alpha_m]).astype(F32)
+    mine = lax.div(jnp.arange(width, dtype=jnp.int32), piece) == index
+    small = jnp.where(mine[None, :], jnp.tile(vectors, (1, width // piece)), 0.0)
+    small = jnp.pad(small, ((0, 13), (0, 0))).astype(BF16)
+    vmem = pl.BlockSpec(memory_space=pltpu.VMEM)
+    bf = lambda *shape: pltpu.VMEM(shape, BF16)
+    fl = lambda *shape: pltpu.VMEM(shape, F32)
+    out_shapes = [
+        ((256, 1024), BF16), ((256, 1024), BF16), ((32, 3072), F32), ((32, 1024), F32),
+        ((128, 1024), F32), ((128, 1024), F32), ((128, 1024), F32), ((8, 1024), F32),
+    ]
+    scratch = [
+        bf(1024, 1024), bf(3, 1024, 256), bf(8, 4, 32, 1024), bf(1024, 1024), bf(1024, 1024),
+        bf(1024, 1024), bf(3, 16, 1024), bf(8, 16, 1024), fl(16, 1024),
+        fl(2, 1024, 256), bf(3, 1024, 256), fl(1024, 256), bf(1024, 256), bf(4, 256, 256),
+        fl(256, 1024), fl(256, 1024), bf(1024, 1024), bf(1024, 1024), bf(1024, 1024), bf(1024, 1024),
+        bf(1024, 1024), bf(3, 256, 1024), bf(3, 256, 1024), bf(3, 256, 1024),
+        fl(256, 1024), fl(256, 1024), bf(1024, 1024), bf(256, 1024), bf(3, 256, 256),
+        bf(1024, 256), bf(3, 1024, 256), fl(4, 8, 256),
+        bf(1024, 1024), bf(4, 128, 1024), bf(4, 128, 1024), bf(4, 128, 1024), bf(4, 3, 128, 256),
+        bf(4, 32, 1024), bf(3, 128, 1024), bf(3, 128, 1024), bf(3, 128, 1024), bf(3, 3, 128, 256),
+        bf(3, 32, 1024), bf(256, 1024), bf(256, 1024), bf(256, 1024), bf(256, 1024),
+        fl(3, 128, 256), fl(4, 3, 32, 256), fl(8, 1024), fl(3, 8, 1024), fl(2, 8, 1024), fl(4, 8, 1024),
+        pltpu.SemaphoreType.DMA((COPIES,)), pltpu.SemaphoreType.DMA((COPIES,)),
+    ]
+    outs = pl.pallas_call(
+        fused_kernel,
+        out_shape=[jax.ShapeDtypeStruct(shape, kind) for shape, kind in out_shapes],
+        in_specs=[vmem] * 11,
+        out_specs=[vmem] * 8,
+        scratch_shapes=scratch,
+        compiler_params=pltpu.CompilerParams(
+            collective_id=0, has_side_effects=True, vmem_limit_bytes=VMEM_BYTES
+        ),
+        cost_estimate=pl.CostEstimate(
+            flops=27_000_000_000, bytes_accessed=8_000_000, transcendentals=10_000_000
+        ),
+    )(
+        tokens, cotangent, whole_row,
+        w_qkv.reshape(piece, 3, width).transpose(1, 0, 2), w_out, small, w_up, w_gate, w_down,
+        s_u.astype(F32)[None, :], s_v.astype(F32)[None, :],
+    )
+    result, d_tokens, g_qkv, g_out, g_up, g_gate, g_down, stats = outs
+    own = lax.dynamic_slice(stats, (0, index * piece), (3, piece))
+    entries = n_rows * width * lax.axis_size("dp") * lax.axis_size("tensor")
+    stream_rms = jnp.sqrt(jnp.sum(stats[3:6], axis=1) / entries)
+    return (
+        result, d_tokens, g_qkv, g_out, own[2], own[0], own[1], g_up, g_gate, g_down,
+        stats[6], stats[7], stream_rms,
+    )
+
+
 def solution(mesh):
+    body = fused if fits(mesh) else local
     return jax.shard_map(
-        local,
+        body,
         mesh=mesh,
         in_specs=(
             P(("dp", "tensor"), None),

time: 1140 us -> 325 us (0.29)
  waiting for transfers between devices: 695 us -> 0 us
  Pallas kernels: 0 us -> 304 us
  matrix products: 163 us -> 0 us
  blocking collectives: 106 us -> 0 us
  local copies, waits for them, and re-layouts: 81.6 us -> 16.5 us
  other arithmetic: 62.1 us -> 1.86 us
  between operations: 14.9 us -> 2.03 us
    pallas_call x0 -> x1, Pallas kernels: none -> 304 us  [fused(): pl.pallas_call(fused_kernel, out_shape=[jax.ShapeDtypeStruct(shape, kind)...]
    reduce_scatter x7 -> x0, waiting for transfers between devices: 283 us -> none  [the longest x1 90.5 us: local(): lax.psum_scatter(grad_out, ('dp', 'tensor'), scatter_dimension=0, tiled=T...]
    all_gather x9 -> x0, waiting for transfers between devices: 250 us -> none  [the longest x1 45 us: local(): lax.all_gather(w_up, 'dp', axis=0, tiled=True)]
    dot_general x29 -> x0, matrix products: 163 us -> none  [the longest x6 28 us: block_scores(): jnp.einsum('qhd,khd->hqk', query_heads, key_part, preferred_element_type=...]
    unnamed x18 -> x0, waiting for transfers between devices: 162 us -> none
    unnamed x2 -> x0, blocking collectives: 84.1 us -> none
    reduce_sum x13 -> x1, other arithmetic: 29.6 us -> 0.12 us  [fused(): stream_rms = jnp.sqrt(jnp.sum(stats[3:6], axis=1) / entries)]
    unnamed x116 -> x33, local copies, waits for them, and re-layouts: 33.1 us -> 10.1 us
  transfers between devices with their start and end apart: 17 -> 0, of which waited for: 14 -> 0; matrix products, arithmetic and copies ran while one was open for 17% -> 0% of each run, Pallas kernels for 0% -> 0%
where the time goes in v1:
time: 325 us; the launch traced here: 324 us
  Pallas kernels  304 us (94%)
  local copies, waits for them, and re-layouts  16.5 us (5%)
    pallas_call x1, Pallas kernels, fused(): pl.pallas_call(fused_kernel, out_shape=[jax.ShapeDtypeStruct(shape, kind)...  304 us
    unnamed x33, local copies, waits for them, and re-layouts  10.1 us

profile of v1, /device:TPU:0, one launch (start us, length us, event | category | flops | bytes accessed | tf_op | source)
XLA Modules:
  0.0 324.4 jit_solution(16747883018381561016)
XLA Ops:
  0.6 0.0 copy-start.12
  0.7 0.6 copy-done.12
  1.3 0.1 dynamic_slice.6
  1.4 0.6 fusion.1
  3.3 0.6 broadcast_in_dim.26.whole_row
  3.8 0.0 copy-start.9
  3.8 0.0 copy-start.10
  3.8 0.0 copy-start.11
  3.9 0.6 copy-done.9
  4.5 0.0 copy-done.10
  4.5 0.0 copy-done.11
  4.6 0.1 tile.10
  4.7 0.6 pad.5.small
  5.3 1.6 copy.29
  6.9 0.0 copy-start.7
  6.9 0.7 copy-done.7
  7.6 0.0 copy-start.8
  7.6 0.6 broadcast_in_dim.33
  8.2 0.1 copy-done.8
  8.3 0.6 broadcast_in_dim.34
  8.9 304.0 %shard_map.228 = (bf16[256,1024]{1,0:T(8,128)(2,1)}, bf16[256,1024]{1,0:T(8,128)(2,1)}, f32[32,3072]{1,0:T(8,128)}, f32[32,1024]{1,0:T(8,128)}, f32[128,1024]{1,...) custom-call(bf16[256,1024]{1,0:T(8,128)(2,1)} %tokens.1, bf16[256,1024]{1,0:T(8,128)(2,1)} %cotangent.1, ...), custom_call_target="tpu_custom_call" | custom-call | flops 27000000512 | bytes 8000000 | tf_op jit(solution)/shard_map/pallas_call | solution.py:1073
  312.9 0.0 copy-start.6
  312.9 0.8 constant_dynamic-slice_fusion
  313.7 0.5 slice_bitcast_fusion
  314.3 1.4 fusion
  315.7 0.0 copy-done.6
  315.7 0.1 slice_reduce_fusion
  315.8 0.5 multiply_sqrt_fusion
  316.3 0.0 copy-start.3
  316.3 1.9 copy.37
  318.3 0.0 copy-done.3
  318.3 0.0 copy-start.4
  318.3 0.8 copy.38
  319.1 0.4 copy-done.4
  319.5 0.0 copy-start.5
  319.5 0.0 copy-start.2
  319.5 0.7 copy.39
  320.2 0.2 copy-done.5
  320.5 0.7 copy.40
  321.1 0.0 copy-done.2
  321.1 0.0 copy-start.1
  321.1 0.8 copy.41
  321.9 0.4 copy-done.1
  322.3 0.0 copy-start
  322.4 0.8 copy.42
  323.1 0.4 copy-done
  323.6 0.8 copy.43
  (4 shorter events, 0.0 us)
Async XLA Ops:
  0.6 0.7 copy-start.12
  3.8 0.7 copy-start.9
  3.8 0.7 copy-start.10
  3.8 0.7 copy-start.11
  6.9 0.7 copy-start.7
  7.6 0.7 copy-start.8
  312.9 2.8 copy-start.6
  316.3 1.9 copy-start.3
  318.3 1.2 copy-start.4
  319.5 1.0 copy-start.5
  319.5 1.7 copy-start.2
  321.1 1.2 copy-start.1
  322.3 1.2 copy-start

commit v2 on v0

--- a/solution.py
+++ b/solution.py
@@ -1,8 +1,11 @@
+import functools
 import math
 
 import jax
 import jax.numpy as jnp
 from jax import lax
+from jax.experimental import pallas as pl
+from jax.experimental.pallas import tpu as pltpu
 from jax.sharding import PartitionSpec as P
 
 HEAD_DIM = 64
@@ -335,9 +338,1025 @@
     )
 
 
+MESH = pl.DeviceIdType.MESH
+BF16 = jnp.bfloat16
+F32 = jnp.float32
+LOG2E = 1.4426950408889634
+COPIES = 224
+VMEM_BYTES = 63 * 2**20
+CH = 32
+
+
+def nn(left, right):
+    return lax.dot_general(left, right, (((1,), (0,)), ((), ())), preferred_element_type=F32)
+
+
+def nt(left, right):
+    return lax.dot_general(left, right, (((1,), (1,)), ((), ())), preferred_element_type=F32)
+
+
+def tn(left, right):
+    return lax.dot_general(left, right, (((0,), (0,)), ((), ())), preferred_element_type=F32)
+
+
+def flip(index, bits):
+    bit = 1
+    while bit <= bits:
+        if bits & bit:
+            index = index + bit - 2 * bit * lax.rem(lax.div(index, bit), 2)
+        bit *= 2
+    return index
+
+
+def mean_rows(value):
+    return jnp.mean(value, axis=-1, keepdims=True)
+
+
+def rows(start, count=256):
+    return pl.ds(pl.multiple_of(start * count, count), count)
+
+
+def block(r):
+    return pl.ds(r * 256, 256)
+
+
+def fused_kernel(
+    tokens, cotangent, bucket_start, w_qkv, w_out, s_qk, alpha_a, alpha_m, w_up, w_gate, w_down, scale_u,
+    scale_v,
+    layer_hbm, tokens_hbm, qkv_hbm, out_hbm, up_hbm, gate_hbm, down_hbm, stats_out,
+    layer_out, grad_tokens, grad_qkv, grad_out, grad_up, grad_gate, grad_down,
+    tok, cot, wq, wo, wu, wg, wd, small, small_t, small_d, gains,
+    raw, qkv, linv, att, ato, branch, hid, h1, ur, gr, inn,
+    part, from_core3, from_core1, from_y,
+    dr2, dr1, d_inner_f32, db, dba, dat, dao, dqkv, delta,
+    gd, x_down, x_up, x_gate, x_qkv, x_out, z_down, z_up, z_gate, z_qkv, z_out,
+    o_core3, o_core1, o_y, osum, q_sum, q_piece, stats, s_tensor, s_x, s_z,
+    send_sem, recv_sem, local_sem,
+):
+    d = lax.axis_index("dp")
+    t = lax.axis_index("tensor")
+    z = lax.div(d, 2)
+    inner = lax.rem(lax.div(z + 1, 2), 2) == 1
+    core, ynb, diag = (d, flip(t, 1)), (d, flip(t, 2)), (d, flip(t, 3))
+    tensor_peer = {1: core, 2: ynb, 3: diag}
+    xnb = (flip(d, 1), t)
+    z_peer = {m: (flip(d, m), t) for m in (2, 4, 6)}
+
+    barrier = pltpu.get_barrier_semaphore()
+    peers = [core, ynb, diag, xnb] + [z_peer[m] for m in (2, 4, 6)]
+    for peer in peers:
+        pl.semaphore_signal(barrier, inc=1, device_id=peer, device_id_type=MESH)
+
+    issued = []
+    used = [0]
+
+    def number():
+        used[0] += 1
+        return used[0] - 1
+
+    def describe(src, dst, peer, at, to):
+        return pltpu.make_async_remote_copy(
+            src_ref=src,
+            dst_ref=dst,
+            send_sem=send_sem.at[at],
+            recv_sem=recv_sem.at[to],
+            device_id=peer,
+            device_id_type=MESH,
+        )
+
+    def send(src, dst, peer):
+        at = number()
+        copy = describe(src, dst, peer, at, at)
+        copy.start()
+        issued.append(copy)
+        return copy
+
+    waited = set()
+
+    def sent(copy):
+        if id(copy) not in waited:
+            waited.add(id(copy))
+            copy.wait_send()
+
+    locals_ = []
+
+    def bring(src, dst):
+        copy = pltpu.make_async_copy(src, dst, local_sem.at[len(locals_)])
+        copy.start()
+        locals_.append(copy)
+        return copy
+
+    outer = jnp.logical_not(inner)
+
+    class Gather:
+        def __init__(self, src, view):
+            self.src, self.view = src, view
+            self.at6, self.relay_at = number(), number()
+
+        def start_x(self):
+            self.x = [send(self.src, self.view(d), xnb)]
+
+        def start_far(self):
+            self.z = {4: send(self.src, self.view(d), z_peer[4])}
+            self.straight = describe(self.src, self.view(d), z_peer[6], self.at6, self.at6)
+            pl.when(inner)(self.straight.start)
+
+        def start_near(self):
+            self.z[2] = send(self.src, self.view(d), z_peer[2])
+
+        def start_z(self):
+            self.start_far()
+            self.start_near()
+
+        def hop(self):
+            self.z[4].wait_recv()
+            shard = self.view(flip(d, 4))
+            self.relay = describe(shard, shard, z_peer[2], self.relay_at, self.at6)
+            pl.when(inner)(self.relay.start)
+
+        def forward_one(self, m):
+            if m == 2:
+                self.z[2].wait_recv()
+            if m == 6:
+                self.straight.wait_recv()
+            shard = self.view(flip(d, m))
+            self.x.append(send(shard, shard, xnb))
+
+        def forward(self):
+            self.forward_one(2)
+            self.hop()
+            self.forward_one(4)
+            self.forward_one(6)
+
+        def finish(self):
+            for copy in self.x:
+                copy.wait_recv()
+
+        def release(self):
+            for copy in [*self.z.values(), *self.x]:
+                sent(copy)
+            for copy in (self.straight, self.relay):
+                pl.when(inner)(copy.wait_send)
+
+    class GatherPairs(Gather):
+        def __init__(self, src, shard, pair):
+            super().__init__(src, pair)
+            self.shard = shard
+
+        def start_x(self):
+            self.x = [send(self.src, self.shard(d), xnb)]
+
+        def start_far(self):
+            self.x[0].wait_recv()
+            self.src = self.view(d)
+            super().start_far()
+
+    def rows_of(ref, count=128):
+        return lambda index: ref.at[rows(index, count)]
+
+    def pair_of(ref):
+        return lambda index: ref.at[rows(lax.div(index, 2))]
+
+    take_qkv = Gather(wq.at[:, rows(d, 128), :], lambda index: wq.at[:, rows(index, 128), :])
+    take_small = Gather(small_d.at[:, rows(d, 128)], lambda index: small_d.at[:, rows(index, 128)])
+    take_out = Gather(w_out, lambda index: wo.at[index, t])
+    take_up = Gather(w_up, rows_of(wu))
+    take_gate = Gather(w_gate, rows_of(wg))
+    take_down = GatherPairs(w_down, rows_of(wd), pair_of(wd))
+
+    piece = s_qk.shape[1]
+    own_qkv = pl.ds(pl.multiple_of(d * 128 + t * 32, 32), 32)
+
+    def qkv_cols(slot, pair, j):
+        return pl.ds(pl.multiple_of(j * 1024 + slot * 256 + pair * 128, 128), 128)
+
+    def qkv_place(pair, j):
+        return wq.at[pair, own_qkv, j * 128 : j * 128 + 128]
+
+    parts_of_qkv = [(pair, j) for pair in range(2) for j in range(3)]
+    local_qkv = [
+        bring(w_qkv.at[:, qkv_cols(t, pair, j)], qkv_place(pair, j)) for pair, j in parts_of_qkv
+    ]
+    local_tok = bring(tokens, tok.at[block(0)])
+    local_rest = [
+        bring(w_out, wo.at[d, t]),
+        bring(w_up, wu.at[rows(d, 128)]),
+        bring(w_gate, wg.at[rows(d, 128)]),
+        bring(w_down, wd.at[rows(d, 128)]),
+        bring(cotangent, cot),
+    ]
+    place = jnp.where(
+        lax.broadcasted_iota(jnp.int32, (piece, 128), 1)
+        == lax.broadcasted_iota(jnp.int32, (piece, 128), 0) + t * piece,
+        1.0,
+        0.0,
+    ).astype(BF16)
+    small_row = lax.broadcasted_iota(jnp.int32, (16, 128), 0)
+    placed = jnp.zeros((16, 128), F32)
+    for index, vector in enumerate((s_qk, alpha_a, alpha_m)):
+        placed = jnp.where(small_row == index, nn(vector[...], place), placed)
+    small[...] = placed.astype(BF16)
+    stats[...] = jnp.zeros_like(stats)
+    pl.semaphore_wait(barrier, len(peers))
+
+    small_sends = [send(small, small_t.at[r - 1], tensor_peer[r]) for r in (2, 3, 1)]
+    qkv_sends = [
+        send(w_qkv.at[:, qkv_cols(flip(t, r), pair, j)], qkv_place(pair, j), tensor_peer[r])
+        for r in (2, 3, 1)
+        for pair, j in parts_of_qkv
+    ]
+    take_out.start_z()
+    take_down.start_x()
+    take_out.start_x()
+    for copy in small_sends:
+        copy.wait_recv()
+    small_d[:, rows(d, 128)] = small[...] + small_t[0] + small_t[1] + small_t[2]
+    take_small.start_z()
+    take_small.start_x()
+    for copy in local_qkv:
+        copy.wait()
+    for copy in qkv_sends:
+        copy.wait_recv()
+    take_qkv.start_z()
+    take_qkv.start_x()
+    tok_y = send(tokens, tok.at[block(2)], ynb)
+    tok_core = send(tokens, tok.at[block(1)], core)
+    take_up.start_far()
+
+    take_out.forward()
+    take_small.forward()
+    take_qkv.hop()
+    take_qkv.forward_one(4)
+    take_up.start_near()
+    take_up.start_x()
+    take_qkv.forward_one(2)
+    take_qkv.forward_one(6)
+    take_gate.start_far()
+    tok_y.wait_recv()
+    tok_diag = send(tok.at[block(2)], tok.at[block(3)], core)
+    take_small.finish()
+    gains[...] = small_d[...].astype(F32)
+    take_qkv.finish()
+    local_tok.wait()
+    tok_core.wait_recv()
+    tok_diag.wait_recv()
+
+    def gain_pair(pair):
+        gain = gains[0:1, pl.ds(pl.multiple_of(t * 256 + pair * 128, 128), 128)]
+        return jnp.concatenate([gain, gain], axis=1)
+
+    first_head = lax.broadcasted_iota(jnp.int32, (256, 128), 1) < HEAD_DIM
+    same_head = jnp.where(
+        lax.div(lax.broadcasted_iota(jnp.int32, (256, 256), 0), HEAD_DIM)
+        == lax.div(lax.broadcasted_iota(jnp.int32, (256, 256), 1), HEAD_DIM),
+        1.0,
+        0.0,
+    ).astype(BF16)
+
+    def head_sum(value):
+        high = value.astype(BF16)
+        low = (value - high.astype(F32)).astype(BF16)
+        return nn(high, same_head) + nn(low, same_head)
+
+    def qkv_step(r, carry):
+        at = rows(r)
+        x = tok[at, :]
+        for pair in range(2):
+            y = nn(x, wq[pair])
+            qk = y[:, :256]
+            raw[pair, at, :] = qk
+            factor = lax.rsqrt(head_sum(qk * qk) + EPSILON)
+            qkv[pair, at, :256] = (qk * factor * gain_pair(pair)).astype(BF16)
+            qkv[pair, at, 256:] = y[:, 256:].astype(BF16)
+        return carry
+
+    lax.fori_loop(0, 4, qkv_step, 0)
+
+    def true_rows(i):
+        return rows(flip(t, i))
+
+    whole = jnp.where(bucket_start[d * 4] == bucket_start[d * 4 + 2], 1.0, 0.0)
+    row_id = lax.broadcasted_iota(jnp.int32, (256, 256), 0)
+    col_id = lax.broadcasted_iota(jnp.int32, (256, 256), 1)
+    exp_scale = math.sqrt(HEAD_DIM) * LOG2E
+
+    def two_heads(value):
+        zero = jnp.zeros_like(value)
+        return jnp.concatenate(
+            [jnp.where(first_head, value, zero), jnp.where(first_head, zero, value)], axis=0
+        )
+
+    def one_of_two(value):
+        return jnp.where(first_head, value[:256], value[256:])
+
+    causal = jnp.concatenate([col_id <= row_id] * 2, axis=0)
+
+    def attend(i):
+        at = true_rows(i)
+
+        def head_step(pair, carry):
+            q = two_heads(qkv[pair, at, 0:128])
+            acc = jnp.zeros((512, 128), F32)
+            weight = jnp.zeros((512, 1), F32)
+            for j in range(i + 1):
+                key_at = true_rows(j)
+                e = jnp.exp2(nt(q, qkv[pair, key_at, 128:256]) * exp_scale)
+                if j == i:
+                    e = jnp.where(causal, e, 0.0)
+                elif j // 2 != i // 2:
+                    e = e * whole
+                weight = weight + jnp.sum(e, axis=1, keepdims=True)
+                acc = acc + nn(e.astype(BF16), qkv[pair, key_at, 256:384])
+            inverse = 1.0 / weight
+            lanes = rows(pair, 128)
+            linv[at, lanes] = one_of_two(jnp.broadcast_to(inverse, (512, 128)))
+            att[at, lanes] = one_of_two(acc * inverse).astype(BF16)
+            return carry
+
+        lax.fori_loop(0, 2, head_step, 0)
+
+    attend(0)
+    attend(1)
+    take_up.hop()
+    take_up.forward_one(4)
+    take_gate.start_near()
+    take_gate.start_x()
+    take_up.forward_one(2)
+    take_up.forward_one(6)
+    for copy in local_rest[1:]:
+        copy.wait()
+    take_down.start_far()
+    attend(2)
+    attend(3)
+
+    att_sends = [send(att.at[block(r)], ato.at[t], tensor_peer[r]) for r in (2, 3, 1)]
+    ato[t] = att[block(0), :]
+    take_out.finish()
+    local_rest[0].wait()
+    wo_y = send(wo.at[:, t], wo.at[:, t], ynb)
+    wo_core = send(wo.at[:, t], wo.at[:, t], core)
+    wo_y.wait_recv()
+    wo_far = send(wo.at[:, flip(t, 2)], wo.at[:, flip(t, 2)], core)
+    for copy in att_sends:
+        copy.wait_recv()
+    wo_core.wait_recv()
+    wo_far.wait_recv()
+
+    def out_rows(slot, columns):
+        return wo[2 * slot : 2 * slot + 2, :, :, columns].reshape(256, 256)
+
+    def out_step(n, carry):
+        at = rows(n)
+        acc = nn(ato[0], out_rows(0, at))
+        for slot in range(1, 4):
+            acc = acc + nn(ato[slot], out_rows(slot, at))
+        branch[:, at] = acc
+        return carry
+
+    lax.fori_loop(0, 4, out_step, 0)
+
+    mix_a = gains[1:2, :]
+    mix_m = gains[2:3, :]
+
+    def add_stat(row, value):
+        stats[row : row + 1, :] = stats[row : row + 1, :] + jnp.sum(value, axis=0, keepdims=True)
+
+    def first_norm(at):
+        x = tok[at, :].astype(F32)
+        ba = branch[at, :]
+        fa = lax.rsqrt(mean_rows(ba * ba) + EPSILON)
+        ha = ba * fa
+        r1 = x + mix_a * (ha - x)
+        f1 = lax.rsqrt(mean_rows(r1 * r1) + EPSILON)
+        return x, ba, fa, ha, f1, r1 * f1
+
+    def norm_step(c, carry):
+        at = rows(c, CH)
+        _, ba, _, _, _, hidden = first_norm(at)
+        add_stat(3, ba * ba)
+        hid[at, :] = hidden
+        h1[at, :] = hidden.astype(BF16)
+        return carry
+
+    lax.fori_loop(0, 256 // CH, norm_step, 0)
+
+    def spread(ref):
+        return send(ref.at[block(0)], ref.at[block(2)], ynb), send(
+            ref.at[block(0)], ref.at[block(1)], core
+        )
+
+    def relay(ref, from_ynb):
+        from_ynb.wait_recv()
+        return send(ref.at[block(2)], ref.at[block(3)], core)
+
+    h1_y, h1_core = spread(h1)
+    take_gate.hop()
+    take_gate.forward_one(4)
+    take_down.start_near()
+    take_gate.forward_one(2)
+    take_gate.forward_one(6)
+    h1_far = relay(h1, h1_y)
+    take_up.finish()
+    h1_core.wait_recv()
+    h1_far.wait_recv()
+    take_gate.finish()
+
+    def up_step(r, carry):
+        at = rows(r)
+        hidden = h1[at, :]
+        u_raw = nn(hidden, wu[...])
+        g_raw = nn(hidden, wg[...])
+        gate = g_raw * scale_v[...].astype(F32)
+        silu = gate / (1.0 + jnp.exp(-gate))
+        ur[at, :] = u_raw.astype(BF16)
+        gr[at, :] = g_raw.astype(BF16)
+        inn[at, :] = (u_raw * scale_u[...].astype(F32) * silu).astype(BF16)
+        return carry
+
+    lax.fori_loop(0, 4, up_step, 0)
+
+    class Reduce:
+        def __init__(self, which, before, make):
+            self.which, self.before, self.make = which, before, make
+            self.copies = {}
+
+        def run(self, order):
+            for r in order:
+                self.step(r)
+
+        def step(self, r):
+            k = self.which
+            if r in self.before.copies:
+                before = self.before.copies[r]
+                for copy in before if isinstance(before, list) else [before]:
+                    sent(copy)
+            self.make(r)
+            if r == 3:
+                self.copies[3] = send(part.at[block(3)], from_core3.at[k], core)
+            elif r == 2:
+                self.copies[3].wait_recv()
+                part[block(2), :] = (
+                    part[block(2), :].astype(F32) + from_core3[k].astype(F32)
+                ).astype(BF16)
+                self.copies[2] = send(part.at[block(2)], from_y.at[k], ynb)
+            elif r == 1:
+                self.copies[1] = send(part.at[block(1)], from_core1.at[k], core)
+
+        def finish(self):
+            self.copies[1].wait_recv()
+            self.copies[2].wait_recv()
+
+        def at(self, where):
+            k = self.which
+            return (
+                part[where, :].astype(F32)
+                + from_core1[k, where, :].astype(F32)
+                + from_y[k, where, :].astype(F32)
+            )
+
+    class ReduceColumns:
+        def __init__(self):
+            self.copies = {r: [] for r in (1, 2, 3)}
+            self.columns = []
+
+        def step(self, k):
+            cols = rows(lax.div(flip(d, 2 * k), 2))
+            part[:, cols] = nt(inn[...], wd[cols, :]).astype(BF16)
+            self.columns.append(cols)
+            self.copies[3].append(send(part.at[block(3), cols], from_core3.at[0, :, cols], core))
+            self.copies[1].append(send(part.at[block(1), cols], from_core1.at[0, :, cols], core))
+
+        def pass_on(self):
+            done = len(self.copies[2])
+            cols = self.columns[done]
+            self.copies[3][done].wait_recv()
+            part[block(2), cols] = (
+                part[block(2), cols].astype(F32) + from_core3[0, :, cols].astype(F32)
+            ).astype(BF16)
+            self.copies[2].append(send(part.at[block(2), cols], from_y.at[0, :, cols], ynb))
+
+        def finish(self):
+            for r in (1, 2):
+                for copy in self.copies[r]:
+                    copy.wait_recv()
+
+        at = Reduce.at
+        which = 0
+
+    sum_m = ReduceColumns()
+    sum_m.step(0)
+    take_down.z[2].wait_recv()
+    take_down.hop()
+    sum_m.pass_on()
+    sum_m.step(1)
+    sum_m.pass_on()
+    sum_m.step(2)
+    sum_m.pass_on()
+    take_down.straight.wait_recv()
+    sum_m.step(3)
+    sum_m.pass_on()
+    sum_m.finish()
+
+    def loss_step(c, carry):
+        at = rows(c, CH)
+        bm = sum_m.at(at)
+        hidden = hid[at, :]
+        fm = lax.rsqrt(mean_rows(bm * bm) + EPSILON)
+        hm = bm * fm
+        r2 = hidden + mix_m * (hm - hidden)
+        f2 = lax.rsqrt(mean_rows(r2 * r2) + EPSILON)
+        result = r2 * f2
+        layer_out[at, :] = result.astype(BF16)
+        up = cot[at, :].astype(F32)
+        grad = f2 * (up - result * mean_rows(up * result))
+        dr2[at, :] = grad
+        add_stat(1, grad * (hm - hidden))
+        add_stat(4, bm * bm)
+        add_stat(5, r2 * r2)
+        c_m = mix_m * grad
+        db[at, :] = (fm * (c_m - hm * mean_rows(c_m * hm))).astype(BF16)
+        return carry
+
+    lax.fori_loop(0, 256 // CH, loss_step, 0)
+
+    db_y, db_core = spread(db)
+
+    class AlongZ:
+        def __init__(self, view, landing):
+            self.view, self.landing = view, landing
+            self.at6, self.relay_at = number(), number()
+            self.z = {}
+
+        def push(self, k):
+            shard = self.view(flip(d, 2 * k))
+            if k == 3:
+                self.straight = describe(
+                    shard, self.landing.at[2], z_peer[6], self.at6, self.at6
+                )
+                self.relay = describe(
+                    shard, self.landing.at[3], z_peer[2], self.relay_at, self.relay_at
+                )
+                pl.when(inner)(self.straight.start)
+                pl.when(outer)(self.relay.start)
+            elif k == 2:
+
+                @pl.when(inner)
+                def _():
+                    self.relay.wait_recv()
+                    shard[...] = (shard[...].astype(F32) + self.landing[3].astype(F32)).astype(BF16)
+
+                self.z[2] = send(shard, self.landing.at[1], z_peer[4])
+            else:
+                self.z[1] = send(shard, self.landing.at[0], z_peer[2])
+
+        def total_into(self, out):
+            self.z[1].wait_recv()
+            self.z[2].wait_recv()
+            out[...] = (
+                self.view(d)[...].astype(F32)
+                + self.landing[0].astype(F32)
+                + self.landing[1].astype(F32)
+            ).astype(out.dtype)
+
+            @pl.when(inner)
+            def _():
+                self.straight.wait_recv()
+                out[...] = (out[...].astype(F32) + self.landing[2].astype(F32)).astype(out.dtype)
+
+        def settle(self):
+            pl.when(inner)(self.straight.wait_send)
+            pl.when(outer)(self.relay.wait_send)
+
+    class Scatter(AlongZ):
+        def __init__(self, view, from_x, landing):
+            super().__init__(view, landing)
+            self.from_x = from_x
+            self.x = {}
+
+        def ship(self, k):
+            self.x[k] = send(self.view(flip(d, 2 * k + 1)), self.from_x.at[k], xnb)
+
+        def fold(self, k):
+            self.x[k].wait_recv()
+            own = self.view(flip(d, 2 * k))
+            own[...] = (own[...].astype(F32) + self.from_x[k].astype(F32)).astype(BF16)
+            if k in (1, 3):
+                self.push(k)
+
+    def weight_grad(left, right, out, ship):
+        for k in (3, 1, 2, 0):
+            at = rows(lax.div(flip(d, 2 * k), 2))
+
+            out[at, :] = tn(left[:, at], right[...]).astype(BF16)
+            ship(k)
+
+    def make_hidden(r):
+        at = block(r)
+        d_inner_f32[...] = nn(db[at, :], wd[...])
+
+        def inner_step(c, carry):
+            here = rows(c, CH)
+            where = pl.ds(pl.multiple_of(r * 256 + c * CH, CH), CH)
+            d_inner = d_inner_f32[here, :]
+            u_raw = ur[where, :].astype(F32)
+            g_raw = gr[where, :].astype(F32)
+            gain_u = scale_u[...].astype(F32)
+            gain_v = scale_v[...].astype(F32)
+            gate = g_raw * gain_v
+            sig = 1.0 / (1.0 + jnp.exp(-gate))
+            up = u_raw * gain_u
+            d_up = d_inner * (gate * sig)
+            d_gate = d_inner * up * (sig * (1.0 + gate * (1.0 - sig)))
+            add_stat(6, d_up * u_raw)
+            add_stat(7, d_gate * g_raw)
+            ur[where, :] = (d_up * gain_u).astype(BF16)
+            gr[where, :] = (d_gate * gain_v).astype(BF16)
+            return carry
+
+        lax.fori_loop(0, 256 // CH, inner_step, 0)
+        part[at, :] = (nt(ur[at, :], wu[...]) + nt(gr[at, :], wg[...])).astype(BF16)
+
+    sum_h = Reduce(1, sum_m, make_hidden)
+    db_core.wait_recv()
+    sum_h.run((1, 0))
+    db_far = relay(db, db_y)
+    db_far.wait_recv()
+    sum_down = AlongZ(pair_of(gd), z_down)
+    weight_grad(db, inn, gd, lambda k: sum_down.push(k) if k in (1, 3) else None)
+    sum_h.run((3, 2))
+    sum_down.push(2)
+
+    gu, gg, go = wd, wu, wg
+    for gather in (take_down, take_up, take_gate):
+        gather.release()
+    sum_up = Scatter(rows_of(gu), x_up, z_up)
+    sum_gate = Scatter(rows_of(gg), x_gate, z_gate)
+    weight_grad(h1, ur, gu, sum_up.ship)
+    weight_grad(h1, gr, gg, sum_gate.ship)
+    sum_h.finish()
+
+    def mid_step(c, carry):
+        at = rows(c, CH)
+        x, _, fa, ha, f1, hidden = first_norm(at)
+        d_hidden = (1.0 - mix_m) * dr2[at, :] + sum_h.at(at)
+        grad = f1 * (d_hidden - hidden * mean_rows(d_hidden * hidden))
+        dr1[at, :] = grad
+        add_stat(0, grad * (ha - x))
+        c_a = mix_a * grad
+        dba[at, :] = (fa * (c_a - ha * mean_rows(c_a * ha))).astype(BF16)
+        return carry
+
+    lax.fori_loop(0, 256 // CH, mid_step, 0)
+
+    dat_sends = []
+    for r in (2, 3, 1, 0):
+        slot = flip(t, r)
+        weight = wo[pl.ds(2 * slot, 2)].reshape(256, 1024)
+        value = nt(dba[...], weight).astype(BF16)
+        if r:
+            dat[r - 1] = value
+            dat_sends.append(send(dat.at[r - 1], dao.at[block(r)], tensor_peer[r]))
+        else:
+            dao[block(0), :] = value
+    for slot in range(4):
+        g = tn(ato[slot], dba[...]).astype(BF16)
+        for q in range(8):
+            start = (q % 4) * 256 + (2 * slot + q // 4) * 32
+            go[start : start + 32, :] = g[q * 32 : (q + 1) * 32, :]
+
+    def go_rows(r):
+        return rows(flip(t, r))
+
+    go_core3 = send(go.at[go_rows(3)], o_core3, core)
+    go_core1 = send(go.at[go_rows(1)], o_core1, core)
+    go_core3.wait_recv()
+    go[go_rows(2), :] = (go[go_rows(2), :].astype(F32) + o_core3[...].astype(F32)).astype(BF16)
+    go_y = send(go.at[go_rows(2)], o_y, ynb)
+    sum_up.fold(3)
+    sum_up.fold(1)
+
+    head_rows = jnp.where(
+        lax.broadcasted_iota(jnp.int32, (8, 256), 0)
+        == lax.div(lax.broadcasted_iota(jnp.int32, (8, 256), 1), HEAD_DIM),
+        1.0,
+        0.0,
+    ).astype(BF16)
+    for copy in att_sends:
+        sent(copy)
+
+    def ready_step(r, carry):
+        at = rows(r)
+        scaled = (dao[at, :].astype(F32) * linv[at, :]).astype(BF16)
+        dao[at, :] = scaled
+        product = scaled.astype(F32) * att[at, :].astype(F32)
+        high = product.astype(BF16)
+        low = (product - high.astype(F32)).astype(BF16)
+        delta[r] = nt(head_rows, high) + nt(head_rows, low)
+        return carry
+
+    key_grads, query_grads = branch, hid
+    seen = jnp.concatenate([row_id <= col_id] * 2, axis=1)
+
+    def lanes_of(r, half=0):
+        return pl.ds(pl.multiple_of(r * 128 + half * 512, 128), 128)
+
+    def attend_back(pair, query_r, key_r, visible):
+        query_at, key_at = rows(query_r), rows(key_r)
+        q = two_heads(qkv[pair, query_at, 0:128])
+        do = two_heads(dao[query_at, pair * 128 : pair * 128 + 128])
+        keys = qkv[pair, key_at, 128:256]
+        e = visible(jnp.exp2(nt(keys, q) * exp_scale))
+        d_prob = nt(qkv[pair, key_at, 256:384], do)
+        shift = jnp.concatenate(
+            [delta[query_r, 2 * pair + h : 2 * pair + h + 1, :] for h in range(2)], axis=1
+        )
+        d_score = (e * (d_prob - shift)).astype(BF16)
+        key_grads[:, lanes_of(key_r)] += nn(d_score, q)
+        key_grads[:, lanes_of(key_r, 1)] += nn(e.astype(BF16), do)
+        query_grads[:, lanes_of(query_r)] += one_of_two(tn(d_score, keys))
+
+    def diagonal(pair):
+        def diagonal_step(r, carry):
+            attend_back(pair, r, r, lambda e: jnp.where(seen, e, 0.0))
+            return carry
+
+        return diagonal_step
+
+    def mixed(a, b):
+        low = lax.rem(a, 2) + lax.rem(b, 2) - 2 * lax.rem(a, 2) * lax.rem(b, 2)
+        high_a, high_b = lax.div(a, 2), lax.div(b, 2)
+        return low + 2 * (high_a + high_b - 2 * high_a * high_b)
+
+    def below(pair):
+        def below_step(n, carry):
+            i = 1 + lax.div(n, 3) + lax.div(n + 4, 5)
+            j = n - lax.div(i * (i - 1), 2)
+            apart = (lax.div(i, 2) - lax.div(j, 2)).astype(F32)
+            factor = 1.0 - apart + apart * whole
+            attend_back(pair, mixed(i, t), mixed(j, t), lambda e: e * factor)
+            return carry
+
+        return below_step
+
+    def clear():
+        key_grads[...] = jnp.zeros_like(key_grads)
+        query_grads[...] = jnp.zeros_like(query_grads)
+
+    def qkv_back(pair):
+        scale = math.sqrt(HEAD_DIM)
+        gain = gain_pair(pair)
+        column = pl.ds(pl.multiple_of(t * 256 + pair * 128, 128), 128)
+
+        def back_qkv_step(r, carry):
+            at = rows(r)
+            y = raw[pair, at, :]
+            factor = lax.rsqrt(head_sum(y * y) + EPSILON)
+            w = y * factor
+            grad = (
+                jnp.concatenate([query_grads[:, lanes_of(r)], key_grads[:, lanes_of(r)]], axis=1)
+                * scale
+            )
+            both = jnp.sum(grad * w, axis=0, keepdims=True)
+            stats[2:3, column] = stats[2:3, column] + both[:, :128] + both[:, 128:]
+            c = grad * gain
+            dqkv[pair, at, :256] = (factor * (c - w * head_sum(c * w))).astype(BF16)
+            dqkv[pair, at, 256:] = key_grads[:, lanes_of(r, 1)].astype(BF16)
+            return carry
+
+        lax.fori_loop(0, 4, back_qkv_step, 0)
+
+    gq = qkv
+
+    def qkv_shard(pair):
+        return lambda index: gq.at[pair, rows(index, 128), :]
+
+    sum_qkv = [Scatter(qkv_shard(pair), x_qkv.at[pair], z_qkv.at[pair]) for pair in range(2)]
+
+    def qkv_weight(pair):
+        for k in (3, 1, 2, 0):
+            at = rows(lax.div(flip(d, 2 * k), 2))
+            gq[pair, at, :] = tn(tok[:, at], dqkv[pair]).astype(BF16)
+            sum_qkv[pair].ship(k)
+
+    clear()
+    dat_sends[2].wait_recv()
+    lax.fori_loop(0, 2, ready_step, 0)
+    lax.fori_loop(0, 2, diagonal(0), 0)
+    sum_up.fold(2)
+    sum_up.push(2)
+    sum_up.fold(0)
+    dat_sends[0].wait_recv()
+    dat_sends[1].wait_recv()
+    lax.fori_loop(2, 4, ready_step, 0)
+    lax.fori_loop(2, 4, diagonal(0), 0)
+    go_core1.wait_recv()
+    go_y.wait_recv()
+    osum[...] = (
+        go[go_rows(0), :].astype(F32) + o_core1[...].astype(F32) + o_y[...].astype(F32)
+    ).astype(BF16)
+    sum_out = Scatter(rows_of(osum, 32), x_out, z_out)
+    for k in (3, 1, 2, 0):
+        sum_out.ship(k)
+    lax.fori_loop(0, 6, below(0), 0)
+    qkv_back(0)
+    qkv_weight(0)
+    clear()
+    sum_gate.fold(3)
+    sum_gate.fold(1)
+    lax.fori_loop(0, 4, diagonal(1), 0)
+    sum_gate.fold(2)
+    sum_gate.push(2)
+    sum_gate.fold(0)
+    down_pair = pair_of(gd)(d)
+    sum_down.total_into(down_pair)
+    down_x = send(gd.at[rows(flip(d, 1), 128)], x_down, xnb)
+    lax.fori_loop(0, 6, below(1), 0)
+    qkv_back(1)
+    qkv_weight(1)
+    for k in (3, 1, 2, 0):
+        sum_out.fold(k)
+    sum_out.push(2)
+
+    small_back = [send(stats, s_tensor.at[r - 1], tensor_peer[r]) for r in (1, 2, 3)]
+
+    def make_tokens(r):
+        part[block(r), :] = (
+            nt(dqkv[0, block(r), :], wq[0]) + nt(dqkv[1, block(r), :], wq[1])
+        ).astype(BF16)
+
+    sum_t = Reduce(2, sum_h, make_tokens)
+    sum_t.run((3, 2))
+    for k in (3, 1, 2, 0):
+        sum_qkv[0].fold(k)
+    sum_qkv[0].push(2)
+    sum_t.run((1, 0))
+    for copy in small_back:
+        copy.wait_recv()
+    over_tensor = s_tensor[0] + s_tensor[1] + s_tensor[2]
+    shared = lax.broadcasted_iota(jnp.int32, (8, 1024), 0) < 6
+    s_x[0] = stats[...] + jnp.where(shared, over_tensor, 0.0)
+    stat_x = send(s_x.at[0], s_x.at[1], xnb)
+    for k in (3, 1, 2, 0):
+        sum_qkv[1].fold(k)
+    sum_qkv[1].push(2)
+
+    outgoing = []
+
+    def put(src, dst):
+        outgoing.append(bring(src, dst))
+
+    put(layer_out, layer_hbm)
+    down_x.wait_recv()
+    grad_down[...] = gd[rows(d, 128), :].astype(F32) + x_down[...].astype(F32)
+    put(grad_down, down_hbm)
+    sum_up.total_into(grad_up)
+    put(grad_up, up_hbm)
+    sum_gate.total_into(grad_gate)
+    put(grad_gate, gate_hbm)
+    sum_out.total_into(grad_out)
+    put(grad_out, out_hbm)
+    stat_x.wait_recv()
+    s_z[0] = s_x[0] + s_x[1]
+    stat_z = [send(s_z.at[0], s_z.at[k], z_peer[2 * k]) for k in (1, 2, 3)]
+    for pair in range(2):
+        sum_qkv[pair].total_into(q_sum.at[pair])
+    q_sends = [
+        send(q_sum.at[:, rows(flip(t, r), 32), :], q_piece.at[t], tensor_peer[r]) for r in (2, 3, 1)
+    ]
+    q_piece[t] = q_sum[:, rows(t, 32), :]
+    sum_t.finish()
+
+    def last_step(c, carry):
+        at = rows(c, CH)
+        grad_tokens[at, :] = ((1.0 - mix_a) * dr1[at, :] + sum_t.at(at)).astype(BF16)
+        return carry
+
+    lax.fori_loop(0, 256 // CH, last_step, 0)
+    put(grad_tokens, tokens_hbm)
+    for copy in stat_z:
+        copy.wait_recv()
+    stats_out[...] = s_z[0] + s_z[1] + s_z[2] + s_z[3]
+    for copy in q_sends:
+        copy.wait_recv()
+    for slot in range(4):
+        for pair, j in parts_of_qkv:
+            start = j * 1024 + slot * 256 + pair * 128
+            grad_qkv[:, start : start + 128] = q_piece[slot, pair, :, j * 128 : j * 128 + 128]
+    put(grad_qkv, qkv_hbm)
+    for gather in (take_qkv, take_small, take_out):
+        gather.release()
+    for scatter in (sum_down, sum_up, sum_gate, sum_out, *sum_qkv):
+        scatter.settle()
+    for copy in issued:
+        sent(copy)
+    for copy in outgoing:
+        copy.wait()
+
+
+def finish_kernel(entries, *refs):
+    large, stats, outs, held, sems = refs[:7], refs[7], refs[8:18], refs[18:25], refs[25]
+    taken = [pltpu.make_async_copy(large[i], held[i], sems.at[0, i]) for i in range(7)]
+    given = [pltpu.make_async_copy(held[i], outs[i], sems.at[1, i]) for i in range(7)]
+    for copy in taken:
+        copy.start()
+    own, scales, stream = outs[7:]
+    index = lax.axis_index("dp") * lax.axis_size("tensor") + lax.axis_index("tensor")
+    piece = own.shape[1]
+    pick = lax.broadcasted_iota(jnp.int32, (1024, piece), 0) == (
+        lax.broadcasted_iota(jnp.int32, (1024, piece), 1) + index * piece
+    )
+    own[...] = lax.dot_general(
+        stats[0:3, :],
+        jnp.where(pick, 1.0, 0.0),
+        (((1,), (0,)), ((), ())),
+        precision=lax.Precision.HIGHEST,
+        preferred_element_type=F32,
+    )
+    scales[...] = stats[6:8, :]
+    sums = jnp.sum(stats[3:6, :], axis=1, keepdims=True)
+    stream[...] = jnp.broadcast_to(jnp.sqrt(sums / entries), stream.shape)
+    for i in range(7):
+        taken[i].wait()
+        given[i].start()
+    for copy in given:
+        copy.wait()
+
+
+def fits(mesh):
+    return dict(mesh.shape) == {"dp": 8, "tensor": 4}
+
+
+def fused(
+    tokens, cotangent, bucket_start, w_qkv, w_out, s_qk, alpha_a, alpha_m, w_up, w_gate, w_down, s_u, s_v
+):
+    n_rows, width = tokens.shape
+    piece = s_qk.shape[0]
+    vmem = pl.BlockSpec(memory_space=pltpu.VMEM)
+    smem = pl.BlockSpec(memory_space=pltpu.SMEM)
+    hbm = pl.BlockSpec(memory_space=pl.ANY)
+    bf = lambda *shape: pltpu.VMEM(shape, BF16)
+    fl = lambda *shape: pltpu.VMEM(shape, F32)
+    large = [
+        jax.ShapeDtypeStruct(shape, kind)
+        for shape, kind in (
+            ((256, 1024), BF16), ((256, 1024), BF16), ((32, 3072), F32), ((32, 1024), F32),
+            ((128, 1024), F32), ((128, 1024), F32), ((128, 1024), F32),
+        )
+    ]
+    scratch = [
+        *[pltpu.VMEM(leaf.shape, leaf.dtype) for leaf in large],
+        bf(1024, 1024), bf(256, 1024), bf(2, 1024, 384), bf(8, 4, 32, 1024), bf(1024, 1024),
+        bf(1024, 1024), bf(1024, 1024), bf(16, 128), bf(3, 16, 128), bf(16, 1024), fl(16, 1024),
+        fl(2, 1024, 256), bf(2, 1024, 384), fl(1024, 256), bf(1024, 256), bf(4, 256, 256),
+        fl(256, 1024), fl(256, 1024), bf(1024, 1024), bf(1024, 1024), bf(1024, 1024), bf(1024, 1024),
+        bf(1024, 1024), bf(3, 256, 1024), bf(3, 256, 1024), bf(3, 256, 1024),
+        fl(256, 1024), fl(256, 1024), fl(256, 1024), bf(1024, 1024), bf(256, 1024), bf(3, 256, 256),
+        bf(1024, 256), bf(2, 1024, 384), fl(4, 8, 256),
+        bf(1024, 1024), bf(128, 1024), bf(4, 128, 1024), bf(4, 128, 1024), bf(2, 4, 128, 384),
+        bf(4, 32, 1024), bf(4, 256, 1024), bf(4, 128, 1024), bf(4, 128, 1024), bf(2, 4, 128, 384),
+        bf(4, 32, 1024), bf(256, 1024), bf(256, 1024), bf(256, 1024), bf(256, 1024),
+        fl(2, 128, 384), fl(4, 2, 32, 384), fl(8, 1024), fl(3, 8, 1024), fl(2, 8, 1024), fl(4, 8, 1024),
+        pltpu.SemaphoreType.DMA((COPIES,)), pltpu.SemaphoreType.DMA((COPIES,)),
+        pltpu.SemaphoreType.DMA((32,)),
+    ]
+    *big, stats = pl.pallas_call(
+        fused_kernel,
+        out_shape=[*large, jax.ShapeDtypeStruct((8, 1024), F32)],
+        in_specs=[hbm, hbm, smem, hbm, hbm, vmem, vmem, vmem, hbm, hbm, hbm, vmem, vmem],
+        out_specs=[*[hbm] * 7, vmem],
+        scratch_shapes=scratch,
+        compiler_params=pltpu.CompilerParams(
+            collective_id=0, has_side_effects=True, vmem_limit_bytes=VMEM_BYTES
+        ),
+        cost_estimate=pl.CostEstimate(
+            flops=27_000_000_000, bytes_accessed=8_000_000, transcendentals=10_000_000
+        ),
+    )(
+        tokens, cotangent, bucket_start, w_qkv, w_out, s_qk[None, :], alpha_a[None, :],
+        alpha_m[None, :], w_up, w_gate, w_down, s_u[None, :], s_v[None, :],
+    )
+    entries = n_rows * width * lax.axis_size("dp") * lax.axis_size("tensor")
+    *big, own, scales, stream = pl.pallas_call(
+        functools.partial(finish_kernel, float(entries)),
+        out_shape=[
+            *large,
+            jax.ShapeDtypeStruct((3, piece), F32),
+            jax.ShapeDtypeStruct((2, 1024), F32),
+            jax.ShapeDtypeStruct((3, 128), F32),
+        ],
+        in_specs=[hbm] * 7 + [vmem],
+        out_specs=[hbm] * 7 + [vmem] * 3,
+        scratch_shapes=[*[pltpu.VMEM(leaf.shape, leaf.dtype) for leaf in large], pltpu.SemaphoreType.DMA((2, 7))],
+    )(*big, stats)
+    return (
+        *big[:4], own[2], own[0], own[1], *big[4:], scales[0], scales[1], stream[:, 0],
+    )
+
+
 def solution(mesh):
+    body = fused if fits(mesh) else local
     return jax.shard_map(
-        local,
+        body,
         mesh=mesh,
         in_specs=(
             P(("dp", "tensor"), None),

time: 1140 us -> 258 us (0.23)
  waiting for transfers between devices: 695 us -> 0 us
  Pallas kernels: 0 us -> 253 us
  matrix products: 163 us -> 0 us
  blocking collectives: 106 us -> 0 us
  local copies, waits for them, and re-layouts: 81.6 us -> 4.37 us
  other arithmetic: 62.1 us -> 0 us
  between operations: 14.9 us -> 0.7 us
    reduce_scatter x7 -> x0, waiting for transfers between devices: 283 us -> none  [the longest x1 90.5 us: local(): lax.psum_scatter(grad_out, ('dp', 'tensor'), scatter_dimension=0, tiled=T...]
    pallas_call x0 -> x2, Pallas kernels: none -> 253 us  [the longest x1 248 us: fused(): pl.pallas_call(fused_kernel, out_shape=[*large, jax.ShapeDtypeStruct((8,...]
    all_gather x9 -> x0, waiting for transfers between devices: 250 us -> none  [the longest x1 45 us: local(): lax.all_gather(w_up, 'dp', axis=0, tiled=True)]
    dot_general x29 -> x0, matrix products: 163 us -> none  [the longest x6 28 us: block_scores(): jnp.einsum('qhd,khd->hqk', query_heads, key_part, preferred_element_type=...]
    unnamed x18 -> x0, waiting for transfers between devices: 162 us -> none
    unnamed x2 -> x0, blocking collectives: 84.1 us -> none
    unnamed x116 -> x10, local copies, waits for them, and re-layouts: 33.1 us -> 1.43 us
    reduce_sum x13 -> x0, other arithmetic: 29.6 us -> none  [the longest x2 8.99 us: stat_step(): row_total = row_total * jnp.exp(row_top - new_top) + jnp.sum(fresh, axis=-1)]
  transfers between devices with their start and end apart: 17 -> 0, of which waited for: 14 -> 0; matrix products, arithmetic and copies ran while one was open for 17% -> 0% of each run, Pallas kernels for 0% -> 0%
where the time goes in v2:
time: 258 us
  Pallas kernels  253 us (98%)
  local copies, waits for them, and re-layouts  4.37 us (2%)
    pallas_call x1, Pallas kernels, fused(): pl.pallas_call(fused_kernel, out_shape=[*large, jax.ShapeDtypeStruct((8,...  248 us

profile of v2, /device:TPU:0, one launch (start us, length us, event | category | flops | bytes accessed | tf_op | source)
XLA Modules:
  0.0 257.6 jit_solution(1822839178328075286)
XLA Ops:
  0.6 0.0 copy-start.1
  0.7 0.7 copy-done.1
  1.3 0.0 copy-start.2
  1.3 0.6 broadcast_in_dim.18.scale_u
  1.9 0.1 copy-done.2
  2.0 0.6 broadcast_in_dim.19.scale_v
  2.6 248.3 %shard_map.228 = (bf16[256,1024]{1,0:T(8,128)(2,1)}, bf16[256,1024]{1,0:T(8,128)(2,1)}, f32[32,3072]{1,0:T(8,128)}, f32[32,1024]{1,0:T(8,128)}, f32[128,1024]{1,...) custom-call(bf16[256,1024]{1,0:T(8,128)(2,1)} %tokens.1, bf16[256,1024]{1,0:T(8,128)(2,1)} %cotangent.1, ...), custom_call_target="tpu_custom_call" | custom-call | flops 27000000512 | bytes 8000000 | tf_op jit(solution)/shard_map/pallas_call | solution.py:1322
  251.0 4.2 %shard_map.229 = (bf16[256,1024]{1,0:T(8,128)(2,1)}, bf16[256,1024]{1,0:T(8,128)(2,1)}, f32[32,3072]{1,0:T(8,128)}, f32[32,1024]{1,0:T(8,128)}, f32[128,1024]{1,...) custom-call(bf16[256,1024]{1,0:T(8,128)(2,1)} %get-tuple-element.31., ...), custom_call_target="tpu_custom_call" | custom-call | tf_op jit(solution)/shard_map/pallas_call | solution.py:1339
  255.2 0.0 copy-start.3
  255.2 0.0 copy-start.4
  255.2 0.0 copy-start
  255.2 0.7 copy-done.3
  255.8 0.6 slice_reduce_fusion
  256.5 0.0 copy-done.4
  256.5 0.5 slice_bitcast_fusion
  257.0 0.0 copy-done
  257.0 0.6 fusion
Async XLA Ops:
  0.6 0.7 copy-start.1
  1.3 0.7 copy-start.2
  255.2 0.7 copy-start.3
  255.2 1.3 copy-start.4
  255.2 1.8 copy-start
